TPU v7x, 32 devices: a whole 2x2x4 slice. The times are simulated.
32 devices in a mesh: groups: 2 (over y), adapter: 16 (over z, x, core).
Axes of the slice: x: 2, y: 2, z: 4, core: 2. Of those that a mesh axis runs over, the one named last changes fastest.
Arguments:
- tokens: bfloat16 [1024, 8, 3200], P(('groups', 'adapter')), parts along dimension 0, may hold values from -40 to 40
- request_block_adapter: int32 [1024], P(('groups', 'adapter')), parts along dimension 0, may hold values from 0 to 127, as said below
- request_block_rows: int32 [1024], P(('groups', 'adapter')), parts along dimension 0, may hold values from 1 to 8
- adapter_down_weight: bfloat16 [128, 3200, 64], P('adapter'), may hold values from -0.109375 to 0.109375
- adapter_up_weight: bfloat16 [128, 64, 3200], P('adapter'), may hold values from -0.75 to 0.75
Outputs:
- mixed: bfloat16 [1024, 8, 3200], P(('groups', 'adapter')), parts along dimension 0
There are 2 independent parts, one for each index of `groups`. A program takes and returns all parts, laid end to end along the dimension named above; an argument that names none is the same for every part. Nothing has to cross between parts.
Inputs may be any that keep to these rules, and one draw needn't show every extreme that they name: `request_block_adapter`: adapter a is held by the device of index a // 8. The 32 blocks of one device go to at most 8 blocks for each holding device; in every draw some devices receive exactly 8 blocks from every device.
All inputs are finite; a program needn't handle non-finite values.
Results may differ from a plain program's by a relative error of at most 0.0031.
Values may be sent and summed in bfloat16 or wider, within the bound.
No kernel may reach another device: no remote copies, remote signals or barrier semaphores. Data moves between devices by JAX's collectives and lax.ppermute only.
A program may use at most 64 MiB of HBM per device.

v0:
```python
import functools

import jax
import jax.numpy as jnp
from jax import lax
from jax.experimental import pallas as pl
from jax.experimental.pallas import tpu as pltpu
from jax.sharding import PartitionSpec as P

LANES = 128
HALF = 64
QUAD = 4
QUARTER = 32
STEP = 16
NOTE = 96
DOWN_HALVED = (2, 3)
UP_HALVED = (2,)
VMEM = pl.BlockSpec(memory_space=pltpu.VMEM)
SMEM = pl.BlockSpec(memory_space=pltpu.SMEM)


def normalise(tokens):
    values = tokens.astype(jnp.float32)
    mean_sq = jnp.mean(values * values, axis=-1, keepdims=True)
    return (values, (values * lax.rsqrt(mean_sq + 1e-06)).astype(jnp.bfloat16))


def resident_update(hidden_state, block_labels, adapter_down_weight, adapter_up_weight):
    feature_width = hidden_state.shape[-1]
    leading = hidden_state.shape[:-1]
    resident_rows, unused_value, inner_rank = adapter_down_weight.shape
    flattened_tokens = hidden_state.reshape(-1, feature_width)
    down_matrix = jnp.einsum(
        "tq,iqg->tig", flattened_tokens, adapter_down_weight, preferred_element_type=jnp.float32
    )
    down_matrix = down_matrix.astype(jnp.bfloat16).reshape(
        flattened_tokens.shape[0], resident_rows * inner_rank
    )
    column_owner = jnp.arange(resident_rows * inner_rank, dtype=jnp.int32) // inner_rank
    picked = block_labels.reshape(-1, 1) == column_owner[None, :]
    down_matrix = jnp.where(picked, down_matrix, jnp.zeros_like(down_matrix))
    lowrank_update = jnp.dot(
        down_matrix,
        adapter_up_weight.reshape(resident_rows * inner_rank, feature_width),
        preferred_element_type=jnp.float32,
    )
    return lowrank_update.astype(jnp.bfloat16).reshape(leading + (feature_width,))


def rows_to_holders(
    tokens, request_block_adapter, request_block_rows, adapter_down_weight, adapter_up_weight
):
    blocks, rows, feature_width = tokens.shape
    devices = lax.axis_size("adapter")
    resident_rows = adapter_down_weight.shape[0]
    slots = max(1, 4 * blocks // devices)
    values, normed = normalise(tokens)
    owner = request_block_adapter // resident_rows
    within = request_block_adapter - owner * resident_rows
    serial = jnp.arange(blocks, dtype=jnp.int32)
    earlier = (owner[:, None] == owner[None, :]) & (serial[None, :] < serial[:, None])
    position = owner * slots + jnp.sum(earlier, axis=1)
    outgoing = (
        jnp.zeros((devices * slots, rows, feature_width), jnp.bfloat16).at[position].set(normed)
    )
    outgoing = outgoing.reshape(devices, slots, rows, feature_width)
    block_labels = jnp.full((devices * slots,), -1, jnp.int32).at[position].set(within)
    block_labels = jnp.broadcast_to(block_labels[:, None], (devices * slots, rows)).reshape(
        devices, slots, rows
    )
    arriving_rows, row_markers = (
        lax.all_to_all(outgoing, "adapter", split_axis=0, concat_axis=0, tiled=True),
        lax.all_to_all(block_labels, "adapter", split_axis=0, concat_axis=0, tiled=True),
    )
    lowrank_update = resident_update(
        arriving_rows, row_markers, adapter_down_weight, adapter_up_weight
    )
    returned = lax.all_to_all(lowrank_update, "adapter", split_axis=0, concat_axis=0, tiled=True)
    mine = returned.reshape(devices * slots, rows, feature_width)[position]
    live = jnp.arange(rows, dtype=jnp.int32)[None, :] < request_block_rows[:, None]
    mixed = values + jnp.where(live[:, :, None], mine.astype(jnp.float32), jnp.float32(0.0))
    return mixed.astype(jnp.bfloat16)


def lanes_of(rows):
    return lax.broadcasted_iota(jnp.int32, (rows, LANES), 1)


def weight_kernel(whole, which, halved, part_ref, group_ref, weight_ref, *out_refs):
    tiles = whole // LANES
    for k, out_ref in zip(which, out_refs):
        j = part_ref[k]
        if k < 2:
            last = weight_ref[:, QUAD * whole :].astype(jnp.float32)
            turned = pltpu.roll(last, lax.rem(LANES - QUARTER * j, LANES), 1)
            inside = lanes_of(last.shape[0]) < QUARTER
            out_ref[:, 0:whole] = weight_ref[:, pl.ds(pl.multiple_of(j * whole, LANES), whole)]
            out_ref[:, whole:] = jnp.where(inside, turned, 0.0).astype(jnp.bfloat16)
            continue
        count = weight_ref.shape[0] // 2 if k in halved else weight_ref.shape[0]
        start = pl.multiple_of(group_ref[0] * count, count) if k in halved else 0
        for t in range(tiles):
            column = pl.multiple_of(j * whole + t * LANES, LANES)
            out_ref[t * count : (t + 1) * count, :] = weight_ref[
                pl.ds(start, count), pl.ds(column, LANES)
            ]
        last = weight_ref[pl.ds(start, count), QUAD * whole :].astype(jnp.float32)
        size = count // QUAD
        owner = lanes_of(size) // QUARTER
        merged = jnp.zeros((size, LANES), jnp.float32)
        for m in range(QUAD):
            shift = lax.rem(LANES + QUARTER * (m - j), LANES)
            turned = pltpu.roll(last[m * size : (m + 1) * size], shift, 1)
            merged = jnp.where(owner == m, turned, merged)
        out_ref[tiles * count :, :] = merged.astype(jnp.bfloat16)


def open_far(far_refs, halved, opened_ref):
    width = opened_ref.shape[2]
    tiles = width // LANES - 1
    places = [(k - 2, 0) for k in (2, 3)] + [(k - 2, 1) for k in halved]
    for ref, (holder, part) in zip(far_refs, places):
        count = opened_ref.shape[1] // 2 if holder + 2 in halved else opened_ref.shape[1]
        base, size = part * count, count // QUAD
        inside = lanes_of(size) < QUARTER
        for t in range(tiles):
            opened_ref[holder, base : base + count, t * LANES : (t + 1) * LANES] = ref[
                t * count : (t + 1) * count, :
            ]
        packed = ref[tiles * count :, :].astype(jnp.float32)
        for m in range(QUAD):
            turned = pltpu.roll(packed, (LANES - QUARTER * m) % LANES, 1) if m else packed
            opened_ref[holder, base + m * size : base + (m + 1) * size, tiles * LANES :] = (
                jnp.where(inside, turned, 0.0).astype(jnp.bfloat16)
            )


def lay_out(resident, adapter_ref, used_ref, most_ref, target_ref, label_ref):
    blocks, total = adapter_ref.shape[1], target_ref.shape[1]
    rows = total // blocks
    adapter, used = adapter_ref[...], used_ref[...]
    down = lax.broadcasted_iota(jnp.int32, (blocks, blocks), 0)
    across = lax.broadcasted_iota(jnp.int32, (blocks, blocks), 1)

    def turned(value):
        return jnp.sum(jnp.where(down == across, value, 0), axis=1, keepdims=True)

    span = resident * QUAD
    quad = jnp.floor((adapter.astype(jnp.float32) + 0.5) * (1.0 / span)).astype(jnp.int32)
    order = adapter * blocks + lax.broadcasted_iota(jnp.int32, (1, blocks), 1)
    quad_down, order_down, used_down = turned(quad), turned(order), turned(used)
    same = quad_down == quad
    ahead = jnp.sum(jnp.where(same & (order < order_down), used, 0), axis=1, keepdims=True)
    within = jnp.sum(jnp.where(same, used, 0), axis=1, keepdims=True)
    most_ref[...] = jnp.broadcast_to(jnp.max(within, axis=0, keepdims=True), most_ref.shape)
    start = quad_down * total + ahead

    block = lax.broadcasted_iota(jnp.int32, (blocks, total), 0)
    row = lax.broadcasted_iota(jnp.int32, (blocks, total), 1) - block * rows
    place = jnp.where((row >= 0) & (row < used_down), start + row + 1, 0)
    target_ref[...] = jnp.sum(place, axis=0, keepdims=True) - 1
    block = lax.broadcasted_iota(jnp.int32, (total, blocks), 1)
    row = lax.broadcasted_iota(jnp.int32, (total, blocks), 0) - block * rows
    label = jnp.where((row >= 0) & (row < rows), adapter - quad * span + 1, 0)
    label_ref[...] = jnp.sum(label.astype(jnp.float32), axis=1, keepdims=True)


def first_pack_kernel(
    whole, cap, resident, adapter_ref, used_ref, tokens_ref, out_ref, target_ref, label_ref, *refs
):
    normed_ref, most_ref = refs
    lay_out(resident, adapter_ref, used_ref, most_ref, target_ref, label_ref)
    pack_kernel(
        whole, cap, 0, most_ref, target_ref, label_ref, tokens_ref, out_ref, normed_ref
    )


def pack_kernel(
    whole, cap, base, most_ref, target_ref, label_ref, tokens_ref, out_ref, normed_ref
):
    values = tokens_ref[...].astype(jnp.float32)
    mean_sq = jnp.mean(values * values, axis=-1, keepdims=True)
    normed_ref[...] = (values * lax.rsqrt(mean_sq + 1e-06)).astype(jnp.bfloat16)
    total = tokens_ref.shape[0]
    quads, tiles = out_ref.shape[0] // QUAD, whole // LANES
    lane = lanes_of(total)
    last = normed_ref[:, QUAD * whole :].astype(jnp.float32)
    label = jnp.where(lane == QUARTER, label_ref[...], 0.0)
    ends = []
    for j in range(QUAD):
        turned = pltpu.roll(last, (LANES - QUARTER * j) % LANES, 1) if j else last
        ends.append(jnp.where(lane < QUARTER, turned, label).astype(jnp.bfloat16))
    most = most_ref[0:1, 0:1].astype(jnp.float32)
    group_lane = lanes_of(QUARTER) // QUARTER
    step_lane = lanes_of(STEP)
    chosen = []
    for q in range(quads):
        place = lax.broadcasted_iota(jnp.int32, (cap, total), 0) + (q * total + base)
        chosen.append(jnp.where(target_ref[...] == place, 1.0, 0.0).astype(jnp.bfloat16))
    chosen = jnp.concatenate(chosen, axis=0)
    notes = [jnp.where(step_lane == NOTE + cap // STEP, most, 0.0)] * quads
    for j in range(QUAD):
        for t in range(tiles):
            column = j * whole + t * LANES
            if t % 2 == 0:
                count = min(2, tiles - t) * LANES
                share = jnp.dot(
                    chosen,
                    normed_ref[:, column : column + count],
                    preferred_element_type=jnp.float32,
                ).astype(jnp.bfloat16)
            for q in range(quads):
                out_ref[q * QUAD + j, t * cap : (t + 1) * cap, :] = share[
                    q * cap : (q + 1) * cap, t % 2 * LANES : (t % 2 + 1) * LANES
                ]
        end_rows = jnp.dot(chosen, ends[j], preferred_element_type=jnp.float32)
        for q in range(quads):
            end = end_rows[q * cap : (q + 1) * cap]
            if j == 0:
                for a in range(cap // STEP):
                    turned = pltpu.roll(end[a * STEP : (a + 1) * STEP], NOTE + a - QUARTER, 1)
                    notes[q] = jnp.where(step_lane == NOTE + a, turned, notes[q])
            padded = jnp.concatenate(
                [end, jnp.zeros((QUAD * QUARTER - cap, LANES), jnp.float32)], axis=0
            )
            merged = padded[0:QUARTER]
            for m in range(1, QUAD):
                turned = pltpu.roll(padded[m * QUARTER : (m + 1) * QUARTER], m * QUARTER, 1)
                merged = jnp.where(group_lane == m, turned, merged)
            out_ref[q * QUAD + j, tiles * cap : tiles * cap + STEP, :] = merged[0:STEP].astype(
                jnp.bfloat16
            )
            out_ref[q * QUAD + j, tiles * cap + STEP :, :] = jnp.where(
                step_lane >= NOTE, notes[q], merged[STEP:]
            ).astype(jnp.bfloat16)


def read_notes(rows_ref, cap, tiles, part_ref, resident, notes_ref, labels_ref, met_ref):
    senders = rows_ref.shape[0]
    for s in range(senders):
        notes_ref[s * STEP : (s + 1) * STEP, :] = rows_ref[s, tiles * cap + STEP :, :]
    steps = labels_ref.shape[0]
    row = lax.broadcasted_iota(jnp.int32, (steps, LANES), 0)
    wanted = jnp.where(lanes_of(steps) == NOTE + row, 1.0, 0.0).astype(jnp.bfloat16)
    labels = lax.dot_general(
        wanted, notes_ref[...], (((1,), (1,)), ((), ())), preferred_element_type=jnp.float32
    )
    labels_ref[...] = labels
    code = jnp.zeros((steps, 1), jnp.float32)
    for h in range(QUAD):
        first = part_ref[h].astype(jnp.float32) + 1.0
        met = jnp.where((labels >= first) & (labels < first + resident), 1.0, 0.0)
        code = code + (1 << h) * jnp.max(met, axis=1, keepdims=True)
    at = lax.broadcasted_iota(jnp.int32, (steps, 1), 0)
    for a in range(cap // STEP):
        met_ref[a] = jnp.max(jnp.where(at == a, code, 0.0)).astype(jnp.int32)


def for_holders(met_ref, first_ref, near_refs, opened_ref, halved, a, step):
    pairs = opened_ref.shape[1] // LANES
    for h in range(QUAD):
        base = first_ref[h].astype(jnp.float32) + 1.0
        firsts = [base + 2.0 * t for t in range(pairs)]
        if h in halved:
            firsts = [
                base + first_ref[QUAD + i].astype(jnp.float32) + 2.0 * t
                for i in range(2)
                for t in range(pairs // 2)
            ]

        @pl.when(lax.rem(met_ref[a] // (1 << h), 2) > 0)
        def _(h=h, firsts=firsts):
            step(near_refs[h] if h < 2 else opened_ref.at[h - 2], firsts)


def down_kernel(first_ref, rows_ref, *refs):
    near_refs, far_refs, out_ref, count_ref = refs[:2], refs[2:6], refs[6], refs[7]
    notes_ref, met_ref, opened_ref, batch_ref, picked_ref, labels_ref = refs[8:]
    senders, width = rows_ref.shape[0], batch_ref.shape[1]
    tiles = width // LANES - 1
    cap = out_ref.shape[0] * STEP
    rank = out_ref.shape[1]
    resident = opened_ref.shape[1] // rank
    dims = (((1,), (1,)), ((), ()))
    read_notes(rows_ref, cap, tiles, first_ref, resident, notes_ref, labels_ref, met_ref)
    notes = notes_ref[...].astype(jnp.float32)
    is_count = lanes_of(senders * STEP) == NOTE + cap // STEP
    count = jnp.max(jnp.where(is_count, notes, 0.0), axis=(0, 1), keepdims=True)
    count_ref[...] = jnp.broadcast_to(count, count_ref.shape).astype(jnp.bfloat16)
    open_far(far_refs, DOWN_HALVED, opened_ref)

    def one(a, carry):
        picked_ref[...] = jnp.zeros(picked_ref.shape, jnp.float32)

        @pl.when(met_ref[a] > 0)
        def _():
            shift = lax.rem(LANES - QUARTER * (a // 2), LANES)
            spot = pl.multiple_of(tiles * cap + lax.rem(a, 2) * STEP, STEP)
            for s in range(senders):
                rows = slice(s * STEP, (s + 1) * STEP)
                for t in range(tiles):
                    at = pl.multiple_of(t * cap + a * STEP, STEP)
                    batch_ref[rows, t * LANES : (t + 1) * LANES] = rows_ref[s, pl.ds(at, STEP), :]
                end = rows_ref[s, pl.ds(spot, STEP), :].astype(jnp.float32)
                batch_ref[rows, tiles * LANES :] = pltpu.roll(end, shift, 1).astype(jnp.bfloat16)
            label = labels_ref[pl.ds(a, 1), :]

            def step(weight_ref, firsts):
                product = lax.dot_general(
                    weight_ref[...], batch_ref[...], dims, preferred_element_type=jnp.float32
                )
                picked = picked_ref[...]
                for t, first in enumerate(firsts):
                    for i in range(2):
                        at = (2 * t + i) * rank
                        picked = jnp.where(
                            label == first + i, product[at : at + rank, :], picked
                        )
                picked_ref[...] = picked

            for_holders(met_ref, first_ref, near_refs, opened_ref, DOWN_HALVED, a, step)

        out_ref[a] = picked_ref[...]
        return carry

    lax.fori_loop(0, cap // STEP, one, 0)


def pair_kernel(own_ref, other_ref, out_ref):
    out_ref[...] = (own_ref[...] + other_ref[...]).astype(jnp.bfloat16)


def up_kernel(first_ref, met_ref, notes_ref, *refs):
    sum_refs, near_refs, far_refs, out_ref = refs[:2], refs[2:4], refs[4:7], refs[7]
    opened_ref, delta_ref, ends_ref, label_ref, twice_ref = refs[8:]
    senders, width = out_ref.shape[0], opened_ref.shape[2]
    tiles = width // LANES - 1
    rank = sum_refs[0].shape[1]
    kept = (out_ref.shape[1] - QUARTER) // tiles
    group_lane = lanes_of(STEP) // QUARTER
    open_far(far_refs, UP_HALVED, opened_ref)
    ends_ref[...] = jnp.zeros(ends_ref.shape, jnp.float32)
    low = jnp.where(lanes_of(senders * STEP) < HALF, 0.0, 1.0)
    rank_row = lax.broadcasted_iota(jnp.int32, (rank, LANES), 0)
    twofold = jnp.where(lax.rem(lanes_of(rank), rank) == rank_row, 1.0, 0.0).astype(jnp.bfloat16)

    note_row = lax.broadcasted_iota(jnp.int32, (LANES, LANES), 0)
    for a in range(kept // STEP):
        wanted = jnp.where(note_row == NOTE + a, 1.0, 0.0).astype(jnp.bfloat16)
        label_ref[a] = jnp.dot(notes_ref[...], wanted, preferred_element_type=jnp.float32) - low
        down = sum_refs[0][a].astype(jnp.float32) + sum_refs[1][a].astype(jnp.float32)
        twice_ref[a] = lax.dot_general(
            down.astype(jnp.bfloat16),
            twofold,
            (((0,), (0,)), ((), ())),
            preferred_element_type=jnp.float32,
        )

    def one(a, carry):
        delta_ref[...] = jnp.zeros(delta_ref.shape, jnp.float32)

        @pl.when(met_ref[a] > 0)
        def _():
            label, twice = label_ref[a], twice_ref[a]

            def step(weight_ref, firsts):
                placed = [jnp.where(label == first, twice, 0.0) for first in firsts]
                placed = jnp.concatenate(placed, axis=1).astype(jnp.bfloat16)
                delta_ref[...] += jnp.dot(
                    placed, weight_ref[...], preferred_element_type=jnp.float32
                )

            for_holders(met_ref, first_ref, near_refs, opened_ref, UP_HALVED, a, step)

        spot = pl.multiple_of(lax.rem(a, 2) * STEP, STEP)
        for s in range(senders):
            rows = slice(s * STEP, (s + 1) * STEP)
            for t in range(tiles):
                at = pl.multiple_of(t * kept + a * STEP, STEP)
                out_ref[s, pl.ds(at, STEP), :] = delta_ref[
                    rows, t * LANES : (t + 1) * LANES
                ].astype(jnp.bfloat16)
            turned = pltpu.roll(delta_ref[rows, tiles * LANES :], QUARTER * (a // 2), 1)
            ends_ref[s, pl.ds(spot, STEP), :] = jnp.where(
                group_lane == a // 2, turned, ends_ref[s, pl.ds(spot, STEP), :]
            )
        return carry

    lax.fori_loop(0, kept // STEP, one, 0)
    for s in range(senders):
        out_ref[s, tiles * kept :, :] = ends_ref[s].astype(jnp.bfloat16)


def mix_kernel(whole, bases, target_ref, tokens_ref, *refs):
    returned_refs, out_ref = refs[:-1], refs[-1]
    total = tokens_ref.shape[0]
    tiles, quads = whole // LANES, returned_refs[0].shape[0] // QUAD
    lane = lanes_of(total)
    chosen = []
    for base, ref in zip(bases, returned_refs):
        kept = (ref.shape[1] - QUARTER) // tiles
        spot = lax.broadcasted_iota(jnp.int32, (total, quads * kept), 1)
        place = spot // kept * total + spot % kept + base
        chosen.append(jnp.where(target_ref[...] == place, 1.0, 0.0).astype(jnp.bfloat16))
    end = jnp.zeros((total, LANES), jnp.float32)
    for j in range(QUAD):
        delta = 0.0
        for choice, ref in zip(chosen, returned_refs):
            kept = choice.shape[1] // quads
            shares = []
            for q in range(quads):
                d = q * QUAD + j
                parts = [ref[d, t * kept : (t + 1) * kept, :] for t in range(tiles)]
                packed = ref[d, tiles * kept :, :].astype(jnp.float32)
                groups = [packed]
                for m in range(1, QUAD):
                    groups.append(pltpu.roll(packed, LANES - QUARTER * m, 1))
                parts.append(jnp.concatenate(groups, axis=0)[0:kept].astype(jnp.bfloat16))
                shares.append(jnp.concatenate(parts, axis=1))
            share = jnp.concatenate(shares, axis=0)
            delta = delta + jnp.dot(choice, share, preferred_element_type=jnp.float32)
        columns = slice(j * whole, (j + 1) * whole)
        out_ref[:, columns] = (
            tokens_ref[:, columns].astype(jnp.float32) + delta[:, 0:whole]
        ).astype(jnp.bfloat16)
        last = delta[:, whole:]
        turned = pltpu.roll(last, QUARTER * j, 1) if j else last
        end = jnp.where((lane >= QUARTER * j) & (lane < QUARTER * (j + 1)), turned, end)
    out_ref[:, QUAD * whole :] = (
        tokens_ref[:, QUAD * whole :].astype(jnp.float32) + end
    ).astype(jnp.bfloat16)


def call(kernel, out_shape, in_specs, flops, moved, after=(), scratch=(), out_specs=None):
    many = isinstance(out_shape, list)
    skipped = len(after)
    body = (lambda *refs: kernel(*refs[skipped:])) if skipped else kernel
    run = pl.pallas_call(
        body,
        out_shape=out_shape,
        in_specs=[pl.BlockSpec(memory_space=pl.ANY)] * skipped + in_specs,
        out_specs=out_specs or ([VMEM] * len(out_shape) if many else VMEM),
        scratch_shapes=scratch,
        compiler_params=pltpu.CompilerParams(vmem_limit_bytes=48 * 2**20),
        cost_estimate=pl.CostEstimate(flops=flops, bytes_accessed=moved, transcendentals=0),
    )
    return functools.partial(run, *after)


def exchange(value):
    return lax.all_to_all(value, "adapter", split_axis=0, concat_axis=0, tiled=True)


def towards(value, k, devices):
    return lax.ppermute(value, "adapter", [(i, i ^ k) for i in range(devices)])


def swapped(value):
    return lax.ppermute(value, "groups", [(0, 1), (1, 0)])


def stand_behind(value, *earlier):
    return pl.pallas_call(
        lambda *refs: None,
        out_shape=jax.ShapeDtypeStruct(value.shape, value.dtype),
        in_specs=[pl.BlockSpec(memory_space=pl.ANY)] * (1 + len(earlier)),
        out_specs=pl.BlockSpec(memory_space=pl.ANY),
        input_output_aliases={0: 0},
    )(value, *earlier)


def first_pack_call(cap, whole, devices, resident, adapter, used, tokens):
    blocks, rows, width = tokens.shape
    total = blocks * rows
    return call(
        functools.partial(first_pack_kernel, whole, cap, resident),
        [
            jax.ShapeDtypeStruct((devices, whole // LANES * cap + QUARTER, LANES), jnp.bfloat16),
            jax.ShapeDtypeStruct((1, total), jnp.int32),
            jax.ShapeDtypeStruct((total, 1), jnp.float32),
        ],
        [VMEM, VMEM, VMEM],
        2 * devices * cap * total * whole,
        2 * (total * width + devices * cap * whole),
        scratch=[pltpu.VMEM((total, width), jnp.bfloat16), pltpu.VMEM((8, LANES), jnp.int32)],
    )(adapter.reshape(1, blocks), used.reshape(1, blocks), tokens.reshape(total, width))


def pack_call(cap, base, whole, devices, target, label, tokens):
    blocks, rows, width = tokens.shape
    total = blocks * rows
    return call(
        functools.partial(pack_kernel, whole, cap, base),
        jax.ShapeDtypeStruct((devices, whole // LANES * cap + QUARTER, LANES), jnp.bfloat16),
        [VMEM, VMEM, VMEM, VMEM],
        2 * devices * cap * total * whole,
        2 * (total * width + devices * cap * whole),
        scratch=[pltpu.VMEM((total, width), jnp.bfloat16)],
    )(jnp.zeros((8, LANES), jnp.int32), target, label, tokens.reshape(total, width))


def down_call(cap, first, arrived, down_weights, after):
    devices = arrived.shape[0]
    columns, share = down_weights[0].shape
    return call(
        down_kernel,
        [
            jax.ShapeDtypeStruct((cap // STEP, HALF, devices * STEP), jnp.float32),
            jax.ShapeDtypeStruct((STEP, LANES), jnp.bfloat16),
            jax.ShapeDtypeStruct((devices * STEP, LANES), jnp.bfloat16),
            jax.ShapeDtypeStruct((8,), jnp.int32),
        ],
        [SMEM] + [VMEM] * (1 + len(down_weights)),
        0,
        0,
        after,
        [
            pltpu.VMEM((2, columns, share), jnp.bfloat16),
            pltpu.VMEM((devices * STEP, share), jnp.bfloat16),
            pltpu.VMEM((HALF, devices * STEP), jnp.float32),
            pltpu.VMEM((8, devices * STEP), jnp.float32),
        ],
        [VMEM, VMEM, VMEM, SMEM],
    )(first, arrived, *down_weights)


def quad_sums(partial, devices):
    pair = call(
        pair_kernel, jax.ShapeDtypeStruct(partial.shape, jnp.bfloat16), [VMEM, VMEM], 0, 0
    )(partial, towards(partial, 1, devices))
    return [pair, towards(pair, 2, devices)]


def up_call(kept, first, met, notes, sums, up_weights):
    devices = notes.shape[0] // STEP
    columns, share = up_weights[0].shape
    shape = (devices, (share // LANES - 1) * kept + QUARTER, LANES)
    return call(
        up_kernel,
        jax.ShapeDtypeStruct(shape, jnp.bfloat16),
        [SMEM, SMEM] + [VMEM] * (3 + len(up_weights)),
        2 * devices * kept * QUAD * columns * share,
        2 * (2 * devices * kept + QUAD * columns) * share,
        scratch=[
            pltpu.VMEM((2, columns, share), jnp.bfloat16),
            pltpu.VMEM((devices * STEP, share), jnp.float32),
            pltpu.VMEM((devices, QUARTER, LANES), jnp.float32),
            *[pltpu.VMEM((kept // STEP, devices * STEP, LANES), jnp.float32)] * 2,
        ],
    )(first, met, notes, *sums, *up_weights)


def back_and_mix(
    kept, more, tokens, target, label, first, met, notes, sums, down_weights, up_weights, *unused
):
    blocks, rows, width = tokens.shape
    total = blocks * rows
    devices = notes.shape[0] // STEP
    whole = up_weights[0].shape[1] - LANES
    pieces = [exchange(up_call(kept, first, met, notes, sums, up_weights))]
    if more:
        outgoing = pack_call(more, kept, whole, devices, target, label, tokens)
        arrived = exchange(outgoing)
        partial, unused_count, notes, met = down_call(more, first, arrived, down_weights, [])
        sums = quad_sums(partial, devices)
        pieces.append(exchange(up_call(more, first, met, notes, sums, up_weights)))
    mixed = call(
        functools.partial(mix_kernel, whole, (0, kept)[: len(pieces)]),
        jax.ShapeDtypeStruct((total, width), jnp.bfloat16),
        [VMEM] * (2 + len(pieces)),
        2 * devices * (kept + more) * total * whole,
        2 * (2 * total * width + devices * (kept + more) * whole),
    )(target.reshape(total, 1), tokens.reshape(total, width), *pieces)
    return mixed.reshape(tokens.shape)


def start_again(
    tokens, target, label, first, met, notes, sums, down_weights, up_weights, *arguments
):
    return rows_to_holders(tokens, *arguments)


def rows_to_quads(
    tokens, request_block_adapter, request_block_rows, adapter_down_weight, adapter_up_weight
):
    blocks, rows, width = tokens.shape
    devices = lax.axis_size("adapter")
    resident, rank, unused_width = adapter_up_weight.shape
    total = blocks * rows
    columns = resident * rank
    whole = width // LANES // QUAD * LANES
    share = whole + LANES
    bf16, i32 = jnp.bfloat16, jnp.int32

    me = lax.axis_index("adapter").astype(i32)
    group = lax.axis_index("groups").astype(i32)
    parts = jnp.bitwise_xor(me % QUAD, jnp.arange(QUAD, dtype=i32))
    halves = jnp.stack([group, 1 - group]) * (resident // 2)
    first = jnp.concatenate([parts * resident, halves]).astype(i32)
    tiles = whole // LANES

    def shares(weight, halved, after):
        shapes = []
        for k in range(QUAD):
            count = columns // 2 if k in halved else columns
            far = (count * tiles + count // QUAD, LANES)
            shapes.append(jax.ShapeDtypeStruct((columns, share) if k < 2 else far, bf16))
        values = call(
            functools.partial(weight_kernel, whole, range(QUAD), halved),
            shapes,
            [SMEM, SMEM, VMEM],
            0,
            QUAD * columns * width,
            after,
        )(parts, group.reshape(1), weight)
        return [values[0]] + [towards(values[k], k, devices) for k in range(1, QUAD)]

    weight = adapter_down_weight.transpose(0, 2, 1).reshape(columns, width)
    down_weights = shares(weight, DOWN_HALVED, [])
    weight = adapter_up_weight.reshape(columns, width)
    up_weights = shares(weight, UP_HALVED, down_weights[:1])
    down_weights[2] = stand_behind(down_weights[2], up_weights[0])
    down_weights += [swapped(down_weights[k]) for k in DOWN_HALVED]
    up_weights += [swapped(up_weights[k]) for k in UP_HALVED]

    caps = [total * 5 // 16, total * 6 // 16, total * 7 // 16]
    cap = caps[-1]
    outgoing, target, label = first_pack_call(
        cap, whole, devices, resident, request_block_adapter, request_block_rows, tokens
    )
    arrived = exchange(outgoing)
    partial, count, notes, met = down_call(cap, first, arrived, down_weights, up_weights[2:3])
    sums = quad_sums(partial, devices)
    count = count[0:1, 0:1]
    most = jnp.maximum(count, swapped(count))[0, 0].astype(jnp.float32)
    branches = [functools.partial(back_and_mix, kept, 0) for kept in caps]
    branches += [functools.partial(back_and_mix, cap, STEP), start_again]
    return lax.switch(
        sum((most > limit).astype(i32) for limit in [*caps, cap + STEP]),
        branches,
        tokens,
        target,
        label,
        first,
        met,
        notes,
        sums,
        down_weights,
        up_weights,
        request_block_adapter,
        request_block_rows,
        adapter_down_weight,
        adapter_up_weight,
    )


def solution(mesh):
    placed = (
        P(("groups", "adapter"), None, None),
        P(("groups", "adapter")),
        P(("groups", "adapter")),
        P("adapter", None, None),
        P("adapter", None, None),
    )

    def per_device(tokens, request_block_adapter, request_block_rows, down_weight, up_weight):
        blocks, rows, width = tokens.shape
        devices = mesh.shape["adapter"]
        slots = max(1, 4 * blocks // devices)
        quads = devices % QUAD == 0 and slots * QUAD >= blocks
        quads = quads and width % (QUAD * LANES) == LANES and up_weight.shape[1] == HALF
        quads = quads and blocks * rows * 7 // 16 == 7 * STEP and mesh.shape["groups"] == 2
        plan = rows_to_quads if quads else rows_to_holders
        return plan(tokens, request_block_adapter, request_block_rows, down_weight, up_weight)

    return jax.shard_map(
        per_device,
        mesh=mesh,
        in_specs=placed,
        out_specs=P(("groups", "adapter"), None, None),
        check_vma=False,
    )
```

profile of v0, /device:TPU:11, one launch (start us, length us, event | category | flops | bytes accessed | tf_op | source)
XLA Modules:
  0.0 185.7 jit_solution(3088021963745999581)
XLA Ops:
  0.0 3.1 %shard_map.62 = (bf16[16,704,128]{2,1,0:T(8,128)(2,1)S(1)}, s32[1,256]{1,0:T(1,128)}, f32[256,1]{1,0:T(8,128)S(1)}) custom-call(s32[1,32]{1,0:T(1,128)} %bitcast.55, s32[1,32]{1,0:T(1,128)} %bitcast.54, bf16[256,3200]{1,0:T(8,128)(2,1)} %bitcast.35), custom_call_target="tpu_custom_call" | custom-call | flops 704643072 | bytes 4390912 | tf_op jit(solution)/shard_map/pallas_call | solution.py:475
  3.2 1.5 copy-done
  4.7 6.6 %all-to-all-start.9 = ((bf16[16,704,128]{2,1,0:T(8,128)(2,1)}), bf16[16,704,128]{2,1,0:T(8,128)(2,1)S(1)}, u32[]{:S(2)}, u32[]{:S(2)}) async-start(bf16[16,704,128]{2,1,0:T(8,128)(2,1)} %copy-done), calls=%async_computation.9 | async-start | bytes 5767168 | tf_op jit(solution)/shard_map/all_to_all | solution.py:451
  11.3 3.3 %shard_map.60 = (bf16[512,896]{1,0:T(8,128)(2,1)S(1)}, bf16[512,896]{1,0:T(8,128)(2,1)}, bf16[1600,128]{1,0:T(8,128)(2,1)S(1)}, bf16[1600,128]{1,0:T(8,128)(2,1)S(1)}) custom-call(s32[4]{0:T(128)S(1)} %iota_xor_fusion.part_ref.refs_1_, s32[1]{0:T(128)} %bitcast.20.group_ref.refs_2_, bf16[512,3200]{1,0:T(8,128)(2,1)} %bitcast.43), custom_call_target="tpu_custom_call" | custom-call | bytes 6553600 | tf_op jit(solution)/shard_map/pallas_call | solution.py:608
  15.2 1.5 collective-permute-start.5
  16.8 1.9 %shard_map.61 = (bf16[512,896]{1,0:T(8,128)(2,1)}, bf16[512,896]{1,0:T(8,128)(2,1)S(1)}, bf16[1600,128]{1,0:T(8,128)(2,1)}, bf16[3200,128]{1,0:T(8,128)(2,1)S(1)}) custom-call(bf16[512,896]{1,0:T(8,128)(2,1)S(1)} %get-tuple-element.209.refs_0_.refs_3_, s32[4]{0:T(128)S(1)} %iota_xor_fusion.part_ref.refs_1_, s32[1]{0:T(128)} %bitcast.20.group_ref.refs_2_, ...), custom_call_target="tpu_custom_call" | custom-call | bytes 6553600 | tf_op jit(solution)/shard_map/pallas_call | solution.py:608
  18.7 1.0 copy-done.5
  20.8 15.9 %collective-permute-done.4.refs_0_ = bf16[1600,128]{1,0:T(8,128)(2,1)S(1)} collective-permute-done((bf16[1600,128]{1,0:T(8,128)(2,1)S(1)}, bf16[1600,128]{1,0:T(8,128)(2,1)S(1)}, u32[]{:S(2)}, u32[]{:S(2)}) %collective-permute-start.4) | collective-permute-done | bytes 409632 | tf_op jit(solution)/shard_map/ppermute | solution.py:455
  37.5 1.2 collective-permute-start.6
  38.7 15.4 %collective-permute-done.5.refs_6_ = bf16[1600,128]{1,0:T(8,128)(2,1)} collective-permute-done((bf16[1600,128]{1,0:T(8,128)(2,1)S(1)}, bf16[1600,128]{1,0:T(8,128)(2,1)}, u32[]{:S(2)}, u32[]{:S(2)}) %collective-permute-start.5) | collective-permute-done | bytes 409632 | tf_op jit(solution)/shard_map/ppermute | solution.py:455
  54.1 1.2 collective-permute-start.7
  55.4 10.6 %collective-permute-done.2.refs_0_ = bf16[1600,128]{1,0:T(8,128)(2,1)} collective-permute-done((bf16[1600,128]{1,0:T(8,128)(2,1)}, bf16[1600,128]{1,0:T(8,128)(2,1)}, u32[]{:S(2)}, u32[]{:S(2)}) %collective-permute-start.2) | collective-permute-done | bytes 409632 | tf_op jit(solution)/shard_map/ppermute | solution.py:455
  66.0 1.9 %collective-permute-start.12 = (bf16[3200,128]{1,0:T(8,128)(2,1)}, bf16[3200,128]{1,0:T(8,128)(2,1)}, u32[]{:S(2)}, u32[]{:S(2)}) collective-permute-start(bf16[3200,128]{1,0:T(8,128)(2,1)} %copy-done.6), channel_id=1, source_target_pairs={{0,3},{1,2},{2,1},{3,0},{4,7},{5,6},{6,5},{7,4},{8,11},{9,10},{10,... | collective-permute-start | bytes 2457608 | tf_op jit(solution)/shard_map/ppermute | solution.py:455
  68.1 8.0 %all-to-all-done.9.refs_2_ = bf16[16,704,128]{2,1,0:T(8,128)(2,1)S(1)} async-done(((bf16[16,704,128]{2,1,0:T(8,128)(2,1)}), bf16[16,704,128]{2,1,0:T(8,128)(2,1)S(1)}, u32[]{:S(2)}, u32[]{:S(2)}) %all-to-all-start.9) | async-done | bytes 2883616 | tf_op jit(solution)/shard_map/all_to_all | solution.py:451
  76.1 10.7 %shard_map.64 = (f32[7,64,256]{2,1,0:T(8,128)S(1)}, bf16[16,128]{1,0:T(8,128)(2,1)S(1)}, bf16[256,128]{1,0:T(8,128)(2,1)S(1)}, s32[8]{0:T(128)S(1)}) custom-call(bf16[1600,128]{1,0:T(8,128)(2,1)} %collective-permute-done.2.refs_0_, s32[6]{0:T(128)S(1)} %pad_add_fusion.refs_1_, bf16[16,704,128]{2,1,0:T(8,128)(2,1)S(1)} %all-to-all-done.9.refs_2_, ...), custom_call_target="tpu_custom_call" | custom-call | tf_op jit(solution)/shard_map/pallas_call | solution.py:505
  87.0 1.7 collective-permute-done.9.other_ref
  89.3 8.4 %collective-permute-done.8 = bf16[1,1]{1,0:T(2,128)(2,1)} collective-permute-done((bf16[1,1]{1,0:T(2,128)(2,1)}, bf16[1,1]{1,0:T(2,128)(2,1)}, u32[]{:S(2)}, u32[]{:S(2)}) %collective-permute-start.8) | collective-permute-done | bytes 34 | tf_op jit(solution)/shard_map/ppermute | solution.py:459
  99.2 85.4 %conditional.1 = (bf16[32,8,3200]{2,1,0:T(8,128)(2,1)S(1)}) conditional(s32[]{:T(128)} %bitcast.28, (s32[1,256]{1,0:T(1,128)S(1)}, bf16[32,8,3200]{2,1,0:T(8,128)(2,1)}, s32[6]{0:T(128)S(1)}, s32[8]{0:T(128)S(1)}, bf16[256,128]{1,0:T(8,128)(2,1)S(1)}, /*index=5*/bf16[7,64,256]{2,1,0:T(8,128)(2,1)S(1)}, ...), branch_computations={%region_0.1_spmd, %region_1.2_spmd, %region_2.3_spmd, %region_3.4_... | conditional | flops 8422162432 | bytes 107582144 | solution.py:638
  100.3 10.3 %branch_2_fun.2 = bf16[16,704,128]{2,1,0:T(8,128)(2,1)S(1)} custom-call(s32[6]{0:T(128)S(1)} %get-tuple-element.157.first_ref, s32[8]{0:T(128)S(1)} %get-tuple-element.158.met_ref, bf16[256,128]{1,0:T(8,128)(2,1)S(1)} %get-tuple-element.159.notes_ref, bf16[7,64,256]{2,1,0:T(8,128)(2,1)S(1)} %get-tuple-element.160.refs_0_, ...), custom_call_target="tpu_custom_call" | custom-call | flops 6576668672 | bytes 10092544 | tf_op jit(solution)/shard_map/cond/branch_2_fun/pallas_call | solution.py:538
  110.6 1.5 copy-done.2
  112.1 5.3 %all-to-all-start.2 = ((bf16[16,704,128]{2,1,0:T(8,128)(2,1)}), bf16[16,704,128]{2,1,0:T(8,128)(2,1)S(1)}, u32[]{:S(2)}, u32[]{:S(2)}) async-start(bf16[16,704,128]{2,1,0:T(8,128)(2,1)} %copy-done.2), calls=%async_computation.2 | async-start | bytes 5767168 | tf_op jit(solution)/shard_map/cond/branch_2_fun/all_to_all | solution.py:451
  118.2 63.5 %all-to-all-done.2.refs_0_ = bf16[16,704,128]{2,1,0:T(8,128)(2,1)S(1)} async-done(((bf16[16,704,128]{2,1,0:T(8,128)(2,1)}), bf16[16,704,128]{2,1,0:T(8,128)(2,1)S(1)}, u32[]{:S(2)}, u32[]{:S(2)}) %all-to-all-start.2) | async-done | bytes 2883616 | tf_op jit(solution)/shard_map/cond/branch_2_fun/all_to_all | solution.py:451
  181.7 2.8 %branch_2_fun.3 = bf16[256,3200]{1,0:T(8,128)(2,1)S(1)} custom-call(s32[256,1]{1,0:T(8,128)S(1)} %copy.20.target_ref, bf16[256,3200]{1,0:T(8,128)(2,1)} %bitcast.38, bf16[16,704,128]{2,1,0:T(8,128)(2,1)S(1)} %all-to-all-done.2.refs_0_), custom_call_target="tpu_custom_call" | custom-call | flops 704643072 | bytes 6029312 | tf_op jit(solution)/shard_map/cond/branch_2_fun/pallas_call | solution.py:567
  184.5 1.2 copy-done.18
  (45 shorter events, 5.3 us)
Async XLA Ops:
  3.2 1.5 copy-start
  4.7 71.4 %all-to-all-start.9 = ((bf16[16,704,128]{2,1,0:T(8,128)(2,1)}), bf16[16,704,128]{2,1,0:T(8,128)(2,1)S(1)}, u32[]{:S(2)}, u32[]{:S(2)}) async-start(bf16[16,704,128]{2,1,0:T(8,128)(2,1)} %copy-done), calls=%async_computation.9 | async-start | bytes 5767168 | tf_op jit(solution)/shard_map/all_to_all | solution.py:451
  11.3 5.5 %copy-start.16 = (bf16[8,64,3200]{2,1,0:T(8,128)(2,1)S(1)}, bf16[8,64,3200]{2,1,0:T(8,128)(2,1)}, u32[]{:S(2)}) copy-start(bf16[8,64,3200]{2,1,0:T(8,128)(2,1)} %param.14) | copy-start | bytes 9830404
  14.6 22.2 %copy-start.8 = (bf16[512,896]{1,0:T(8,128)(2,1)}, bf16[512,896]{1,0:T(8,128)(2,1)S(1)}, u32[]{:S(2)}) copy-start(bf16[512,896]{1,0:T(8,128)(2,1)S(1)} %get-tuple-element.209.refs_0_.refs_3_) | copy-start | bytes 2752516
  14.6 53.5 %collective-permute-start.3 = (bf16[512,896]{1,0:T(8,128)(2,1)}, bf16[512,896]{1,0:T(8,128)(2,1)}, u32[]{:S(2)}, u32[]{:S(2)}) collective-permute-start(bf16[512,896]{1,0:T(8,128)(2,1)} %get-tuple-element.212), channel_id=1, source_target_pairs={{0,1},{1,0},{2,3},{3,2},{4,5},{5,4},{6,7},{7,6},{8,9},{9,8},{10,11... | collective-permute-start | bytes 2752520 | tf_op jit(solution)/shard_map/ppermute | solution.py:455
  15.0 21.8 %collective-permute-start.4 = (bf16[1600,128]{1,0:T(8,128)(2,1)S(1)}, bf16[1600,128]{1,0:T(8,128)(2,1)S(1)}, u32[]{:S(2)}, u32[]{:S(2)}) collective-permute-start(bf16[1600,128]{1,0:T(8,128)(2,1)S(1)} %get-tuple-element.213), channel_id=1, source_target_pairs={{0,2},{1,3},{2,0},{3,1},{4,6},{5,7},{6,4},{7,5},{8,10},{9,11},{10,... | collective-permute-start | bytes 1228808 | tf_op jit(solution)/shard_map/ppermute | solution.py:455
  15.2 38.9 %collective-permute-start.5 = (bf16[1600,128]{1,0:T(8,128)(2,1)S(1)}, bf16[1600,128]{1,0:T(8,128)(2,1)}, u32[]{:S(2)}, u32[]{:S(2)}) collective-permute-start(bf16[1600,128]{1,0:T(8,128)(2,1)S(1)} %get-tuple-element.215), channel_id=1, source_target_pairs={{0,3},{1,2},{2,1},{3,0},{4,7},{5,6},{6,5},{7,4},{8,11},{9,10},{10,... | collective-permute-start | bytes 1228808 | tf_op jit(solution)/shard_map/ppermute | solution.py:455
  18.7 1.0 copy-start.5
  20.5 45.4 %collective-permute-start.2 = (bf16[1600,128]{1,0:T(8,128)(2,1)}, bf16[1600,128]{1,0:T(8,128)(2,1)}, u32[]{:S(2)}, u32[]{:S(2)}) collective-permute-start(bf16[1600,128]{1,0:T(8,128)(2,1)} %get-tuple-element.210), channel_id=1, source_target_pairs={{0,2},{1,3},{2,0},{3,1},{4,6},{5,7},{6,4},{7,5},{8,10},{9,11},{10,... | collective-permute-start | bytes 1228808 | tf_op jit(solution)/shard_map/ppermute | solution.py:455
  37.5 30.6 %collective-permute-start.6 = (bf16[1600,128]{1,0:T(8,128)(2,1)}, bf16[1600,128]{1,0:T(8,128)(2,1)}, u32[]{:S(2)}, u32[]{:S(2)}) collective-permute-start(bf16[1600,128]{1,0:T(8,128)(2,1)} %shard_map.63.refs_5_), channel_id=1, source_target_pairs={{0,16},{16,0},{1,17},{17,1},{2,18},{18,2},{3,19},{19,3},{4,20},{20... | collective-permute-start | bytes 1228808 | tf_op jit(solution)/shard_map/ppermute | solution.py:459
  54.1 14.0 %collective-permute-start.7 = (bf16[1600,128]{1,0:T(8,128)(2,1)}, bf16[1600,128]{1,0:T(8,128)(2,1)}, u32[]{:S(2)}, u32[]{:S(2)}) collective-permute-start(bf16[1600,128]{1,0:T(8,128)(2,1)} %collective-permute-done.5.refs_6_), channel_id=1, source_target_pairs={{0,16},{16,0},{1,17},{17,1},{2,18},{18,2},{3,19},{19,3},{4,20},{20... | collective-permute-start | bytes 1228808 | tf_op jit(solution)/shard_map/ppermute | solution.py:459
  55.4 43.8 %collective-permute-start.11 = (bf16[512,896]{1,0:T(8,128)(2,1)}, bf16[512,896]{1,0:T(8,128)(2,1)}, u32[]{:S(2)}, u32[]{:S(2)}) collective-permute-start(bf16[512,896]{1,0:T(8,128)(2,1)} %copy-done.5), channel_id=1, source_target_pairs={{0,1},{1,0},{2,3},{3,2},{4,5},{5,4},{6,7},{7,6},{8,9},{9,8},{10,11... | collective-permute-start | bytes 2752520 | tf_op jit(solution)/shard_map/ppermute | solution.py:455
  66.0 33.1 %collective-permute-start.12 = (bf16[3200,128]{1,0:T(8,128)(2,1)}, bf16[3200,128]{1,0:T(8,128)(2,1)}, u32[]{:S(2)}, u32[]{:S(2)}) collective-permute-start(bf16[3200,128]{1,0:T(8,128)(2,1)} %copy-done.6), channel_id=1, source_target_pairs={{0,3},{1,2},{2,1},{3,0},{4,7},{5,6},{6,5},{7,4},{8,11},{9,10},{10,... | collective-permute-start | bytes 2457608 | tf_op jit(solution)/shard_map/ppermute | solution.py:455
  68.1 31.1 %copy-start.11 = (bf16[1600,128]{1,0:T(8,128)(2,1)S(1)}, bf16[1600,128]{1,0:T(8,128)(2,1)}, u32[]{:S(2)}) copy-start(bf16[1600,128]{1,0:T(8,128)(2,1)} %shard_map.63.refs_5_) | copy-start | bytes 1228804
  68.1 31.1 %copy-start.19 = (s32[1,256]{1,0:T(1,128)S(1)}, s32[1,256]{1,0:T(1,128)}, u32[]{:S(2)}) copy-start(s32[1,256]{1,0:T(1,128)} %get-tuple-element.217) | copy-start | bytes 3076
  76.1 23.0 %copy-start.12 = (bf16[512,896]{1,0:T(8,128)(2,1)S(1)}, bf16[512,896]{1,0:T(8,128)(2,1)}, u32[]{:S(2)}) copy-start(bf16[512,896]{1,0:T(8,128)(2,1)} %get-tuple-element.214.refs_1_) | copy-start | bytes 2752516
  86.8 1.9 %collective-permute-start.9 = (f32[7,64,256]{2,1,0:T(8,128)S(1)}, f32[7,64,256]{2,1,0:T(8,128)S(1)}, u32[]{:S(2)}, u32[]{:S(2)}) collective-permute-start(f32[7,64,256]{2,1,0:T(8,128)S(1)} %get-tuple-element.220.own_ref), channel_id=1, source_target_pairs={{0,1},{1,0},{2,3},{3,2},{4,5},{5,4},{6,7},{7,6},{8,9},{9,8},{10,11... | collective-permute-start | bytes 1376264 | tf_op jit(solution)/shard_map/ppermute | solution.py:455
  86.9 12.2 %collective-permute-start.13 = (bf16[1600,128]{1,0:T(8,128)(2,1)}, bf16[1600,128]{1,0:T(8,128)(2,1)S(1)}, u32[]{:S(2)}, u32[]{:S(2)}) collective-permute-start(bf16[1600,128]{1,0:T(8,128)(2,1)} %collective-permute-done.2.refs_0_), channel_id=1, source_target_pairs={{0,16},{16,0},{1,17},{17,1},{2,18},{18,2},{3,19},{19,3},{4,20},{20... | collective-permute-start | bytes 1228808 | tf_op jit(solution)/shard_map/ppermute | solution.py:459
  88.7 10.4 %collective-permute-start.10 = (bf16[7,64,256]{2,1,0:T(8,128)(2,1)S(1)}, bf16[7,64,256]{2,1,0:T(8,128)(2,1)S(1)}, u32[]{:S(2)}, u32[]{:S(2)}) collective-permute-start(bf16[7,64,256]{2,1,0:T(8,128)(2,1)S(1)} %shard_map.65), channel_id=1, source_target_pairs={{0,2},{1,3},{2,0},{3,1},{4,6},{5,7},{6,4},{7,5},{8,10},{9,11},{10,... | collective-permute-start | bytes 688136 | tf_op jit(solution)/shard_map/ppermute | solution.py:455
  89.3 8.4 %collective-permute-start.8 = (bf16[1,1]{1,0:T(2,128)(2,1)}, bf16[1,1]{1,0:T(2,128)(2,1)}, u32[]{:S(2)}, u32[]{:S(2)}) collective-permute-start(bf16[1,1]{1,0:T(2,128)(2,1)} %slice.3), channel_id=1, source_target_pairs={{0,16},{16,0},{1,17},{17,1},{2,18},{18,2},{3,19},{19,3},{4,20},{20... | collective-permute-start | bytes 14 | tf_op jit(solution)/shard_map/ppermute | solution.py:459
  99.4 11.2 %copy-start.20 = (s32[1,256]{1,0:T(1,128)}, s32[1,256]{1,0:T(1,128)S(1)}, u32[]{:S(2)}) copy-start(s32[1,256]{1,0:T(1,128)S(1)} %get-tuple-element.155) | copy-start | bytes 3076 | tf_op jit(solution)/shard_map/cond
  110.6 1.5 copy-start.2
  112.1 69.6 %all-to-all-start.2 = ((bf16[16,704,128]{2,1,0:T(8,128)(2,1)}), bf16[16,704,128]{2,1,0:T(8,128)(2,1)S(1)}, u32[]{:S(2)}, u32[]{:S(2)}) async-start(bf16[16,704,128]{2,1,0:T(8,128)(2,1)} %copy-done.2), calls=%async_computation.2 | async-start | bytes 5767168 | tf_op jit(solution)/shard_map/cond/branch_2_fun/all_to_all | solution.py:451
  184.5 1.2 copy-start.18
  (3 other events, 2.6 us)
where the time goes:
time: 186 us
  waiting for transfers between devices  124 us (67%)
  Pallas kernels  32.2 us (17%)
  starting transfers between devices  19 us (10%)
  local copies, waits for them, and re-layouts  9.11 us (5%)
    all_to_all x2, waiting for transfers between devices, exchange(): lax.all_to_all(value, 'adapter', split_axis=0, concat_axis=0, tiled=True)  71.5 us
    ppermute x8, waiting for transfers between devices, towards(): return lax.ppermute(value, 'adapter', [(i, i ^ k) for i in range(devices)])  43.6 us
    all_to_all x2, starting transfers between devices, exchange(): lax.all_to_all(value, 'adapter', split_axis=0, concat_axis=0, tiled=True)  11.9 us
    pallas_call x1, Pallas kernels, down_call(): call(down_kernel, [jax.ShapeDtypeStruct((cap // STEP, HALF, devices * STE...  10.7 us
    pallas_call x1, Pallas kernels, up_call(): call(up_kernel, jax.ShapeDtypeStruct(shape, jnp.bfloat16), [SMEM, SMEM] +...  10.3 us
    ppermute x4, waiting for transfers between devices, swapped(): return lax.ppermute(value, 'groups', [(0, 1), (1, 0)])  8.43 us
    unnamed x20, local copies, waits for them, and re-layouts  5.36 us
    pallas_call x2, Pallas kernels, shares(): call(functools.partial(weight_kernel, whole, range(QUAD), halved), shapes...  5.22 us
  transfers between devices with their start and end apart: 14, of which 7 were waited for; matrix products, arithmetic and copies ran while one was open for 1% of the time, Pallas kernels for 9%

commit v1 on v0

--- a/solution.py
+++ b/solution.py
@@ -13,8 +13,6 @@
 QUARTER = 32
 STEP = 16
 NOTE = 96
-DOWN_HALVED = (2, 3)
-UP_HALVED = (2,)
 VMEM = pl.BlockSpec(memory_space=pltpu.VMEM)
 SMEM = pl.BlockSpec(memory_space=pltpu.SMEM)
 
@@ -86,9 +84,9 @@
     return lax.broadcasted_iota(jnp.int32, (rows, LANES), 1)
 
 
-def weight_kernel(whole, which, halved, part_ref, group_ref, weight_ref, *out_refs):
+def weight_kernel(whole, pieces, part_ref, group_ref, weight_ref, *out_refs):
     tiles = whole // LANES
-    for k, out_ref in zip(which, out_refs):
+    for (k, start, count, halved), out_ref in zip(pieces, out_refs):
         j = part_ref[k]
         if k < 2:
             last = weight_ref[:, QUAD * whole :].astype(jnp.float32)
@@ -97,8 +95,8 @@
             out_ref[:, 0:whole] = weight_ref[:, pl.ds(pl.multiple_of(j * whole, LANES), whole)]
             out_ref[:, whole:] = jnp.where(inside, turned, 0.0).astype(jnp.bfloat16)
             continue
-        count = weight_ref.shape[0] // 2 if k in halved else weight_ref.shape[0]
-        start = pl.multiple_of(group_ref[0] * count, count) if k in halved else 0
+        if halved:
+            start = pl.multiple_of(group_ref[0] * (weight_ref.shape[0] // 2) + start, count)
         for t in range(tiles):
             column = pl.multiple_of(j * whole + t * LANES, LANES)
             out_ref[t * count : (t + 1) * count, :] = weight_ref[
@@ -115,13 +113,11 @@
         out_ref[tiles * count :, :] = merged.astype(jnp.bfloat16)
 
 
-def open_far(far_refs, halved, opened_ref):
+def open_far(far_refs, places, opened_ref):
     width = opened_ref.shape[2]
     tiles = width // LANES - 1
-    places = [(k - 2, 0) for k in (2, 3)] + [(k - 2, 1) for k in halved]
-    for ref, (holder, part) in zip(far_refs, places):
-        count = opened_ref.shape[1] // 2 if holder + 2 in halved else opened_ref.shape[1]
-        base, size = part * count, count // QUAD
+    for ref, (holder, base, count) in zip(far_refs, places):
+        size = count // QUAD
         inside = lanes_of(size) < QUARTER
         for t in range(tiles):
             opened_ref[holder, base : base + count, t * LANES : (t + 1) * LANES] = ref[
@@ -133,6 +129,16 @@
             opened_ref[holder, base + m * size : base + (m + 1) * size, tiles * LANES :] = (
                 jnp.where(inside, turned, 0.0).astype(jnp.bfloat16)
             )
+
+
+def far_places(pieces, rows):
+    far = [piece for piece in pieces if piece[0] >= 2]
+    own = [(k - 2, start, count) for k, start, count, halved in far]
+    return own + [(k - 2, rows // 2 + start, count) for k, start, count, halved in far if halved]
+
+
+def split(pieces):
+    return sorted({k for k, start, count, halved in pieces if halved})
 
 
 def lay_out(resident, adapter_ref, used_ref, most_ref, target_ref, label_ref):
@@ -273,9 +279,9 @@
             step(near_refs[h] if h < 2 else opened_ref.at[h - 2], firsts)
 
 
-def down_kernel(first_ref, rows_ref, *refs):
-    near_refs, far_refs, out_ref, count_ref = refs[:2], refs[2:6], refs[6], refs[7]
-    notes_ref, met_ref, opened_ref, batch_ref, picked_ref, labels_ref = refs[8:]
+def down_kernel(pieces, first_ref, rows_ref, *refs):
+    near_refs, far_refs, (out_ref, count_ref, notes_ref, met_ref) = refs[:2], refs[2:-8], refs[-8:-4]
+    opened_ref, batch_ref, picked_ref, labels_ref = refs[-4:]
     senders, width = rows_ref.shape[0], batch_ref.shape[1]
     tiles = width // LANES - 1
     cap = out_ref.shape[0] * STEP
@@ -287,7 +293,7 @@
     is_count = lanes_of(senders * STEP) == NOTE + cap // STEP
     count = jnp.max(jnp.where(is_count, notes, 0.0), axis=(0, 1), keepdims=True)
     count_ref[...] = jnp.broadcast_to(count, count_ref.shape).astype(jnp.bfloat16)
-    open_far(far_refs, DOWN_HALVED, opened_ref)
+    open_far(far_refs, far_places(pieces, opened_ref.shape[1]), opened_ref)
 
     def one(a, carry):
         picked_ref[...] = jnp.zeros(picked_ref.shape, jnp.float32)
@@ -318,7 +324,7 @@
                         )
                 picked_ref[...] = picked
 
-            for_holders(met_ref, first_ref, near_refs, opened_ref, DOWN_HALVED, a, step)
+            for_holders(met_ref, first_ref, near_refs, opened_ref, split(pieces), a, step)
 
         out_ref[a] = picked_ref[...]
         return carry
@@ -330,15 +336,15 @@
     out_ref[...] = (own_ref[...] + other_ref[...]).astype(jnp.bfloat16)
 
 
-def up_kernel(first_ref, met_ref, notes_ref, *refs):
-    sum_refs, near_refs, far_refs, out_ref = refs[:2], refs[2:4], refs[4:7], refs[7]
-    opened_ref, delta_ref, ends_ref, label_ref, twice_ref = refs[8:]
+def up_kernel(pieces, first_ref, met_ref, notes_ref, *refs):
+    sum_refs, near_refs, far_refs, out_ref = refs[:2], refs[2:4], refs[4:-6], refs[-6]
+    opened_ref, delta_ref, ends_ref, label_ref, twice_ref = refs[-5:]
     senders, width = out_ref.shape[0], opened_ref.shape[2]
     tiles = width // LANES - 1
     rank = sum_refs[0].shape[1]
     kept = (out_ref.shape[1] - QUARTER) // tiles
     group_lane = lanes_of(STEP) // QUARTER
-    open_far(far_refs, UP_HALVED, opened_ref)
+    open_far(far_refs, far_places(pieces, opened_ref.shape[1]), opened_ref)
     ends_ref[...] = jnp.zeros(ends_ref.shape, jnp.float32)
     low = jnp.where(lanes_of(senders * STEP) < HALF, 0.0, 1.0)
     rank_row = lax.broadcasted_iota(jnp.int32, (rank, LANES), 0)
@@ -370,7 +376,7 @@
                     placed, weight_ref[...], preferred_element_type=jnp.float32
                 )
 
-            for_holders(met_ref, first_ref, near_refs, opened_ref, UP_HALVED, a, step)
+            for_holders(met_ref, first_ref, near_refs, opened_ref, split(pieces), a, step)
 
         spot = pl.multiple_of(lax.rem(a, 2) * STEP, STEP)
         for s in range(senders):
@@ -499,11 +505,27 @@
     )(jnp.zeros((8, LANES), jnp.int32), target, label, tokens.reshape(total, width))
 
 
+def down_pieces(rows):
+    quarter, half = rows // 4, rows // 2
+    return [(0, 0, rows, False), (1, 0, rows, False)] + [
+        (2, 0, quarter, True),
+        (2, quarter, quarter, True),
+        (3, 0, half, True),
+    ]
+
+
+def up_pieces(rows):
+    return [(0, 0, rows, False), (1, 0, rows, False)] + [
+        (2, 0, rows // 2, True),
+        (3, 0, rows, False),
+    ]
+
+
 def down_call(cap, first, arrived, down_weights, after):
     devices = arrived.shape[0]
     columns, share = down_weights[0].shape
     return call(
-        down_kernel,
+        functools.partial(down_kernel, down_pieces(columns)),
         [
             jax.ShapeDtypeStruct((cap // STEP, HALF, devices * STEP), jnp.float32),
             jax.ShapeDtypeStruct((STEP, LANES), jnp.bfloat16),
@@ -536,7 +558,7 @@
     columns, share = up_weights[0].shape
     shape = (devices, (share // LANES - 1) * kept + QUARTER, LANES)
     return call(
-        up_kernel,
+        functools.partial(up_kernel, up_pieces(columns)),
         jax.ShapeDtypeStruct(shape, jnp.bfloat16),
         [SMEM, SMEM] + [VMEM] * (3 + len(up_weights)),
         2 * devices * kept * QUAD * columns * share,
@@ -599,36 +621,39 @@
     first = jnp.concatenate([parts * resident, halves]).astype(i32)
     tiles = whole // LANES
 
-    def shares(weight, halved, after):
+    def shares(weight, pieces, after):
         shapes = []
-        for k in range(QUAD):
-            count = columns // 2 if k in halved else columns
+        for k, start, count, halved in pieces:
             far = (count * tiles + count // QUAD, LANES)
             shapes.append(jax.ShapeDtypeStruct((columns, share) if k < 2 else far, bf16))
         values = call(
-            functools.partial(weight_kernel, whole, range(QUAD), halved),
+            functools.partial(weight_kernel, whole, pieces),
             shapes,
             [SMEM, SMEM, VMEM],
             0,
             QUAD * columns * width,
             after,
         )(parts, group.reshape(1), weight)
-        return [values[0]] + [towards(values[k], k, devices) for k in range(1, QUAD)]
-
-    weight = adapter_down_weight.transpose(0, 2, 1).reshape(columns, width)
-    down_weights = shares(weight, DOWN_HALVED, [])
-    weight = adapter_up_weight.reshape(columns, width)
-    up_weights = shares(weight, UP_HALVED, down_weights[:1])
-    down_weights[2] = stand_behind(down_weights[2], up_weights[0])
-    down_weights += [swapped(down_weights[k]) for k in DOWN_HALVED]
-    up_weights += [swapped(up_weights[k]) for k in UP_HALVED]
+        return [
+            towards(value, piece[0], devices) if piece[0] else value
+            for piece, value in zip(pieces, values)
+        ]
+
+    pieces = down_pieces(columns)
+    down_weights = shares(adapter_down_weight.transpose(0, 2, 1).reshape(columns, width), pieces, [])
+    early = down_weights[2]
+    pieces = up_pieces(columns)
+    up_weights = shares(adapter_up_weight.reshape(columns, width), pieces, down_weights[:1])
+    down_weights[3] = stand_behind(down_weights[3], up_weights[0])
+    down_weights += [swapped(value) for value in down_weights[2:]]
+    up_weights.append(swapped(up_weights[2]))
 
     caps = [total * 5 // 16, total * 6 // 16, total * 7 // 16]
     cap = caps[-1]
     outgoing, target, label = first_pack_call(
         cap, whole, devices, resident, request_block_adapter, request_block_rows, tokens
     )
-    arrived = exchange(outgoing)
+    arrived = exchange(stand_behind(outgoing, early))
     partial, count, notes, met = down_call(cap, first, arrived, down_weights, up_weights[2:3])
     sums = quad_sums(partial, devices)
     count = count[0:1, 0:1]

time: 186 us -> 183 us (0.984)
  starting transfers between devices: 19 us -> 32.6 us
  waiting for transfers between devices: 124 us -> 111 us
  Pallas kernels: 32.2 us -> 25.7 us
    ppermute x8 -> x9, waiting for transfers between devices: 43.6 us -> 33.5 us  [towards(): return lax.ppermute(value, 'adapter', [(i, i ^ k) for i in range(devices)])]
    all_to_all x2, waiting for transfers between devices: 71.5 us -> 64 us  [exchange(): lax.all_to_all(value, 'adapter', split_axis=0, concat_axis=0, tiled=True)]
    ppermute x8 -> x9, starting transfers between devices: 4.52 us -> 10.1 us  [towards(): return lax.ppermute(value, 'adapter', [(i, i ^ k) for i in range(devices)])]
    ppermute x4 -> x5, starting transfers between devices: 2.57 us -> 7.9 us  [swapped(): return lax.ppermute(value, 'groups', [(0, 1), (1, 0)])]
    ppermute x4 -> x5, waiting for transfers between devices: 8.43 us -> 13.6 us  [swapped(): return lax.ppermute(value, 'groups', [(0, 1), (1, 0)])]
    pallas_call x4, Pallas kernels: 26.2 us -> 21.2 us  [the longest x1 7.32 us: down_call(): call(functools.partial(down_kernel, down_pieces(columns)), [jax.ShapeDtyp...]
    all_to_all x2, starting transfers between devices: 11.9 us -> 14.5 us  [exchange(): lax.all_to_all(value, 'adapter', split_axis=0, concat_axis=0, tiled=True)]
    unnamed x20 -> x34, local copies, waits for them, and re-layouts: 5.36 us -> 7.62 us
  transfers between devices with their start and end apart: 14 -> 16, of which waited for: 7 -> 8; matrix products, arithmetic and copies ran while one was open for 1% -> 0% of each run, Pallas kernels for 9% -> 7%
where the time goes in v1:
time: 183 us; the launch traced here: 182 us
  waiting for transfers between devices  111 us (61%)
  starting transfers between devices  32.6 us (18%)
  Pallas kernels  25.7 us (14%)
  local copies, waits for them, and re-layouts  10.7 us (6%)
    all_to_all x2, waiting for transfers between devices, exchange(): lax.all_to_all(value, 'adapter', split_axis=0, concat_axis=0, tiled=True)  64 us
    ppermute x9, waiting for transfers between devices, towards(): return lax.ppermute(value, 'adapter', [(i, i ^ k) for i in range(devices)])  33.5 us
    all_to_all x2, starting transfers between devices, exchange(): lax.all_to_all(value, 'adapter', split_axis=0, concat_axis=0, tiled=True)  14.5 us
    ppermute x5, waiting for transfers between devices, swapped(): return lax.ppermute(value, 'groups', [(0, 1), (1, 0)])  13.6 us
    ppermute x9, starting transfers between devices, towards(): return lax.ppermute(value, 'adapter', [(i, i ^ k) for i in range(devices)])  10.1 us
    ppermute x5, starting transfers between devices, swapped(): return lax.ppermute(value, 'groups', [(0, 1), (1, 0)])  7.9 us
    unnamed x34, local copies, waits for them, and re-layouts  7.62 us
    pallas_call x1, Pallas kernels, down_call(): call(functools.partial(down_kernel, down_pieces(columns)), [jax.ShapeDtyp...  7.32 us
  transfers between devices with their start and end apart: 16, of which 8 were waited for; matrix products, arithmetic and copies ran while one was open for 0% of the time, Pallas kernels for 7%

profile of v1, /device:TPU:11, one launch (start us, length us, event | category | flops | bytes accessed | tf_op | source)
XLA Modules:
  0.0 182.1 jit_solution(10863797427840928593)
XLA Ops:
  0.0 3.3 %shard_map.60 = (bf16[512,896]{1,0:T(8,128)(2,1)}, bf16[512,896]{1,0:T(8,128)(2,1)S(1)}, bf16[800,128]{1,0:T(8,128)(2,1)S(1)}, bf16[800,128]{1,0:T(8,128)(2,1)S(1)}, bf16[1600,128]{1,0:T(8,128)(2,1)S(1)}) custom-call(s32[4]{0:T(128)S(1)} %iota_xor_fusion.part_ref.refs_1_, s32[1]{0:T(128)} %bitcast.20.group_ref.refs_2_, bf16[512,3200]{1,0:T(8,128)(2,1)} %bitcast.43), custom_call_target="tpu_custom_call" | custom-call | bytes 6553600 | tf_op jit(solution)/shard_map/pallas_call | solution.py:629
  4.5 1.7 shard_map.62
  6.2 1.5 copy-done
  7.8 2.4 %collective-permute-done.3.refs_1_.refs_5_ = bf16[800,128]{1,0:T(8,128)(2,1)S(1)} collective-permute-done((bf16[800,128]{1,0:T(8,128)(2,1)S(1)}, bf16[800,128]{1,0:T(8,128)(2,1)S(1)}, u32[]{:S(2)}, u32[]{:S(2)}) %collective-permute-start.3) | collective-permute-done | bytes 204832 | tf_op jit(solution)/shard_map/ppermute | solution.py:461
  10.9 7.4 %all-to-all-start.9 = ((bf16[16,704,128]{2,1,0:T(8,128)(2,1)}), bf16[16,704,128]{2,1,0:T(8,128)(2,1)S(1)}, u32[]{:S(2)}, u32[]{:S(2)}) async-start(bf16[16,704,128]{2,1,0:T(8,128)(2,1)} %shard_map.63), calls=%async_computation.9 | async-start | bytes 5767168 | tf_op jit(solution)/shard_map/all_to_all | solution.py:457
  20.2 3.3 %shard_map.61 = (bf16[512,896]{1,0:T(8,128)(2,1)}, bf16[512,896]{1,0:T(8,128)(2,1)S(1)}, bf16[1600,128]{1,0:T(8,128)(2,1)}, bf16[3200,128]{1,0:T(8,128)(2,1)S(1)}) custom-call(bf16[512,896]{1,0:T(8,128)(2,1)} %get-tuple-element.216.refs_0_.refs_3_, s32[4]{0:T(128)S(1)} %iota_xor_fusion.part_ref.refs_1_, s32[1]{0:T(128)} %bitcast.20.group_ref.refs_2_, ...), custom_call_target="tpu_custom_call" | custom-call | bytes 6553600 | tf_op jit(solution)/shard_map/pallas_call | solution.py:629
  25.7 26.4 %collective-permute-done.5.refs_0_ = bf16[800,128]{1,0:T(8,128)(2,1)S(1)} collective-permute-done((bf16[800,128]{1,0:T(8,128)(2,1)S(1)}, bf16[800,128]{1,0:T(8,128)(2,1)S(1)}, u32[]{:S(2)}, u32[]{:S(2)}) %collective-permute-start.5) | collective-permute-done | bytes 204832 | tf_op jit(solution)/shard_map/ppermute | solution.py:461
  54.2 1.9 %collective-permute-start.13 = (bf16[512,896]{1,0:T(8,128)(2,1)}, bf16[512,896]{1,0:T(8,128)(2,1)}, u32[]{:S(2)}, u32[]{:S(2)}) collective-permute-start(bf16[512,896]{1,0:T(8,128)(2,1)} %copy-done.5), channel_id=1, source_target_pairs={{0,1},{1,0},{2,3},{3,2},{4,5},{5,4},{6,7},{7,6},{8,9},{9,8},{10,11... | collective-permute-start | bytes 2752520 | tf_op jit(solution)/shard_map/ppermute | solution.py:461
  56.2 2.2 %collective-permute-done.8.refs_9_ = bf16[800,128]{1,0:T(8,128)(2,1)S(1)} collective-permute-done((bf16[800,128]{1,0:T(8,128)(2,1)}, bf16[800,128]{1,0:T(8,128)(2,1)S(1)}, u32[]{:S(2)}, u32[]{:S(2)}) %collective-permute-start.8) | collective-permute-done | bytes 204832 | tf_op jit(solution)/shard_map/ppermute | solution.py:465
  58.3 5.7 %collective-permute-start.14 = (bf16[3200,128]{1,0:T(8,128)(2,1)}, bf16[3200,128]{1,0:T(8,128)(2,1)}, u32[]{:S(2)}, u32[]{:S(2)}) collective-permute-start(bf16[3200,128]{1,0:T(8,128)(2,1)} %copy-done.7), channel_id=1, source_target_pairs={{0,3},{1,2},{2,1},{3,0},{4,7},{5,6},{6,5},{7,4},{8,11},{9,10},{10,... | collective-permute-start | bytes 2457608 | tf_op jit(solution)/shard_map/ppermute | solution.py:461
  64.0 4.7 %collective-permute-done.2.refs_0_ = bf16[1600,128]{1,0:T(8,128)(2,1)} collective-permute-done((bf16[1600,128]{1,0:T(8,128)(2,1)}, bf16[1600,128]{1,0:T(8,128)(2,1)}, u32[]{:S(2)}, u32[]{:S(2)}) %collective-permute-start.2) | collective-permute-done | bytes 409632 | tf_op jit(solution)/shard_map/ppermute | solution.py:461
  68.7 1.2 collective-permute-start.7
  70.1 4.1 %collective-permute-done.7.refs_8_ = bf16[800,128]{1,0:T(8,128)(2,1)S(1)} collective-permute-done((bf16[800,128]{1,0:T(8,128)(2,1)}, bf16[800,128]{1,0:T(8,128)(2,1)S(1)}, u32[]{:S(2)}, u32[]{:S(2)}) %collective-permute-start.7) | collective-permute-done | bytes 204832 | tf_op jit(solution)/shard_map/ppermute | solution.py:465
  74.9 8.3 %all-to-all-done.9.refs_2_ = bf16[16,704,128]{2,1,0:T(8,128)(2,1)S(1)} async-done(((bf16[16,704,128]{2,1,0:T(8,128)(2,1)}), bf16[16,704,128]{2,1,0:T(8,128)(2,1)S(1)}, u32[]{:S(2)}, u32[]{:S(2)}) %all-to-all-start.9) | async-done | bytes 2883616 | tf_op jit(solution)/shard_map/all_to_all | solution.py:457
  83.2 7.3 %shard_map.65 = (f32[7,64,256]{2,1,0:T(8,128)S(1)}, bf16[16,128]{1,0:T(8,128)(2,1)S(1)}, bf16[256,128]{1,0:T(8,128)(2,1)S(1)}, s32[8]{0:T(128)S(1)}) custom-call(bf16[1600,128]{1,0:T(8,128)(2,1)} %collective-permute-done.2.refs_0_, s32[6]{0:T(128)S(1)} %pad_add_fusion.refs_1_, bf16[16,704,128]{2,1,0:T(8,128)(2,1)S(1)} %all-to-all-done.9.refs_2_, ...), custom_call_target="tpu_custom_call" | custom-call | tf_op jit(solution)/shard_map/pallas_call | solution.py:527
  90.6 3.5 %collective-permute-start.15 = (bf16[1600,128]{1,0:T(8,128)(2,1)}, bf16[1600,128]{1,0:T(8,128)(2,1)S(1)}, u32[]{:S(2)}, u32[]{:S(2)}) collective-permute-start(bf16[1600,128]{1,0:T(8,128)(2,1)} %collective-permute-done.2.refs_0_), channel_id=1, source_target_pairs={{0,16},{16,0},{1,17},{17,1},{2,18},{18,2},{3,19},{19,3},{4,20},{20... | collective-permute-start | bytes 1228808 | tf_op jit(solution)/shard_map/ppermute | solution.py:465
  94.7 1.7 collective-permute-start.10
  96.5 7.3 %collective-permute-done.10 = bf16[1,1]{1,0:T(2,128)(2,1)} collective-permute-done((bf16[1,1]{1,0:T(2,128)(2,1)}, bf16[1,1]{1,0:T(2,128)(2,1)}, u32[]{:S(2)}, u32[]{:S(2)}) %collective-permute-start.10) | collective-permute-done | bytes 34 | tf_op jit(solution)/shard_map/ppermute | solution.py:465
  105.1 75.9 %conditional.1 = (bf16[32,8,3200]{2,1,0:T(8,128)(2,1)S(1)}) conditional(s32[]{:T(128)} %bitcast.28, (s32[1,256]{1,0:T(1,128)S(1)}, bf16[32,8,3200]{2,1,0:T(8,128)(2,1)}, s32[6]{0:T(128)S(1)}, s32[8]{0:T(128)S(1)}, bf16[256,128]{1,0:T(8,128)(2,1)S(1)}, /*index=5*/bf16[7,64,256]{2,1,0:T(8,128)(2,1)S(1)}, ...), branch_computations={%region_0.1_spmd, %region_1.2_spmd, %region_2.3_spmd, %region_3.4_... | conditional | flops 8422162432 | bytes 107582144 | solution.py:663
  106.1 7.3 %branch_1_fun.2 = bf16[16,608,128]{2,1,0:T(8,128)(2,1)S(1)} custom-call(s32[6]{0:T(128)S(1)} %get-tuple-element.149.first_ref, s32[8]{0:T(128)S(1)} %get-tuple-element.150.met_ref, bf16[256,128]{1,0:T(8,128)(2,1)S(1)} %get-tuple-element.151.notes_ref, bf16[7,64,256]{2,1,0:T(8,128)(2,1)S(1)} %get-tuple-element.152.refs_0_, ...), custom_call_target="tpu_custom_call" | custom-call | flops 5637144576 | bytes 9175040 | tf_op jit(solution)/shard_map/cond/branch_1_fun/pallas_call | solution.py:560
  113.3 1.4 copy-done.3
  114.8 7.1 %all-to-all-start.1 = ((bf16[16,608,128]{2,1,0:T(8,128)(2,1)}), bf16[16,608,128]{2,1,0:T(8,128)(2,1)S(1)}, u32[]{:S(2)}, u32[]{:S(2)}) async-start(bf16[16,608,128]{2,1,0:T(8,128)(2,1)} %copy-done.3), calls=%async_computation.1 | async-start | bytes 4980736 | tf_op jit(solution)/shard_map/cond/branch_1_fun/all_to_all | solution.py:457
  122.0 55.7 %all-to-all-done.1.refs_0_ = bf16[16,608,128]{2,1,0:T(8,128)(2,1)S(1)} async-done(((bf16[16,608,128]{2,1,0:T(8,128)(2,1)}), bf16[16,608,128]{2,1,0:T(8,128)(2,1)S(1)}, u32[]{:S(2)}, u32[]{:S(2)}) %all-to-all-start.1) | async-done | bytes 2490400 | tf_op jit(solution)/shard_map/cond/branch_1_fun/all_to_all | solution.py:457
  177.7 2.7 %branch_1_fun.3 = bf16[256,3200]{1,0:T(8,128)(2,1)S(1)} custom-call(s32[256,1]{1,0:T(8,128)S(1)} %copy.20.target_ref, bf16[256,3200]{1,0:T(8,128)(2,1)} %bitcast.37, bf16[16,608,128]{2,1,0:T(8,128)(2,1)S(1)} %all-to-all-done.1.refs_0_), custom_call_target="tpu_custom_call" | custom-call | flops 603979776 | bytes 5636096 | tf_op jit(solution)/shard_map/cond/branch_1_fun/pallas_call | solution.py:589
  (62 shorter events, 12.0 us)
Async XLA Ops:
  0.0 4.5 %copy-start.31 = (s32[32]{0:T(128)S(1)}, s32[32]{0:T(128)}, u32[]{:S(2)}) copy-start(s32[32]{0:T(128)} %param.12) | copy-start | bytes 388
  0.0 4.5 %copy-start.8 = (bf16[32,8,3200]{2,1,0:T(8,128)(2,1)S(1)}, bf16[32,8,3200]{2,1,0:T(8,128)(2,1)}, u32[]{:S(2)}) copy-start(bf16[32,8,3200]{2,1,0:T(8,128)(2,1)} %param.10) | copy-start | bytes 4915204
  4.3 5.9 %collective-permute-start.3 = (bf16[800,128]{1,0:T(8,128)(2,1)S(1)}, bf16[800,128]{1,0:T(8,128)(2,1)S(1)}, u32[]{:S(2)}, u32[]{:S(2)}) collective-permute-start(bf16[800,128]{1,0:T(8,128)(2,1)S(1)} %get-tuple-element.219), channel_id=1, source_target_pairs={{0,2},{1,3},{2,0},{3,1},{4,6},{5,7},{6,4},{7,5},{8,10},{9,11},{10,... | collective-permute-start | bytes 614408 | tf_op jit(solution)/shard_map/ppermute | solution.py:461
  10.9 72.3 %all-to-all-start.9 = ((bf16[16,704,128]{2,1,0:T(8,128)(2,1)}), bf16[16,704,128]{2,1,0:T(8,128)(2,1)S(1)}, u32[]{:S(2)}, u32[]{:S(2)}) async-start(bf16[16,704,128]{2,1,0:T(8,128)(2,1)} %shard_map.63), calls=%async_computation.9 | async-start | bytes 5767168 | tf_op jit(solution)/shard_map/all_to_all | solution.py:457
  18.3 56.6 %collective-permute-start.4 = (bf16[512,896]{1,0:T(8,128)(2,1)}, bf16[512,896]{1,0:T(8,128)(2,1)}, u32[]{:S(2)}, u32[]{:S(2)}) collective-permute-start(bf16[512,896]{1,0:T(8,128)(2,1)} %copy-done.6), channel_id=1, source_target_pairs={{0,1},{1,0},{2,3},{3,2},{4,5},{5,4},{6,7},{7,6},{8,9},{9,8},{10,11... | collective-permute-start | bytes 2752520 | tf_op jit(solution)/shard_map/ppermute | solution.py:461
  18.7 35.3 %collective-permute-start.6 = (bf16[1600,128]{1,0:T(8,128)(2,1)S(1)}, bf16[1600,128]{1,0:T(8,128)(2,1)}, u32[]{:S(2)}, u32[]{:S(2)}) collective-permute-start(bf16[1600,128]{1,0:T(8,128)(2,1)S(1)} %get-tuple-element.223), channel_id=1, source_target_pairs={{0,3},{1,2},{2,1},{3,0},{4,7},{5,6},{6,5},{7,4},{8,11},{9,10},{10,... | collective-permute-start | bytes 1228808 | tf_op jit(solution)/shard_map/ppermute | solution.py:461
  19.0 33.0 %collective-permute-start.5 = (bf16[800,128]{1,0:T(8,128)(2,1)S(1)}, bf16[800,128]{1,0:T(8,128)(2,1)S(1)}, u32[]{:S(2)}, u32[]{:S(2)}) collective-permute-start(bf16[800,128]{1,0:T(8,128)(2,1)S(1)} %get-tuple-element.221), channel_id=1, source_target_pairs={{0,2},{1,3},{2,0},{3,1},{4,6},{5,7},{6,4},{7,5},{8,10},{9,11},{10,... | collective-permute-start | bytes 614408 | tf_op jit(solution)/shard_map/ppermute | solution.py:461
  25.4 43.3 %collective-permute-start.2 = (bf16[1600,128]{1,0:T(8,128)(2,1)}, bf16[1600,128]{1,0:T(8,128)(2,1)}, u32[]{:S(2)}, u32[]{:S(2)}) collective-permute-start(bf16[1600,128]{1,0:T(8,128)(2,1)} %get-tuple-element.217), channel_id=1, source_target_pairs={{0,2},{1,3},{2,0},{3,1},{4,6},{5,7},{6,4},{7,5},{8,10},{9,11},{10,... | collective-permute-start | bytes 1228808 | tf_op jit(solution)/shard_map/ppermute | solution.py:461
  52.8 5.5 %collective-permute-start.8 = (bf16[800,128]{1,0:T(8,128)(2,1)}, bf16[800,128]{1,0:T(8,128)(2,1)S(1)}, u32[]{:S(2)}, u32[]{:S(2)}) collective-permute-start(bf16[800,128]{1,0:T(8,128)(2,1)} %shard_map.64.refs_6_), channel_id=1, source_target_pairs={{0,16},{16,0},{1,17},{17,1},{2,18},{18,2},{3,19},{19,3},{4,20},{20... | collective-permute-start | bytes 614408 | tf_op jit(solution)/shard_map/ppermute | solution.py:465
  54.0 20.2 %collective-permute-start.9 = (bf16[1600,128]{1,0:T(8,128)(2,1)}, bf16[1600,128]{1,0:T(8,128)(2,1)}, u32[]{:S(2)}, u32[]{:S(2)}) collective-permute-start(bf16[1600,128]{1,0:T(8,128)(2,1)} %collective-permute-done.6.refs_7_), channel_id=1, source_target_pairs={{0,16},{16,0},{1,17},{17,1},{2,18},{18,2},{3,19},{19,3},{4,20},{20... | collective-permute-start | bytes 1228808 | tf_op jit(solution)/shard_map/ppermute | solution.py:465
  54.2 50.7 %collective-permute-start.13 = (bf16[512,896]{1,0:T(8,128)(2,1)}, bf16[512,896]{1,0:T(8,128)(2,1)}, u32[]{:S(2)}, u32[]{:S(2)}) collective-permute-start(bf16[512,896]{1,0:T(8,128)(2,1)} %copy-done.5), channel_id=1, source_target_pairs={{0,1},{1,0},{2,3},{3,2},{4,5},{5,4},{6,7},{7,6},{8,9},{9,8},{10,11... | collective-permute-start | bytes 2752520 | tf_op jit(solution)/shard_map/ppermute | solution.py:461
  58.3 11.7 %copy-start.21 = (bf16[800,128]{1,0:T(8,128)(2,1)}, bf16[800,128]{1,0:T(8,128)(2,1)S(1)}, u32[]{:S(2)}) copy-start(bf16[800,128]{1,0:T(8,128)(2,1)S(1)} %collective-permute-done.8.refs_9_) | copy-start | bytes 614404
  58.3 46.7 %collective-permute-start.14 = (bf16[3200,128]{1,0:T(8,128)(2,1)}, bf16[3200,128]{1,0:T(8,128)(2,1)}, u32[]{:S(2)}, u32[]{:S(2)}) collective-permute-start(bf16[3200,128]{1,0:T(8,128)(2,1)} %copy-done.7), channel_id=1, source_target_pairs={{0,3},{1,2},{2,1},{3,0},{4,7},{5,6},{6,5},{7,4},{8,11},{9,10},{10,... | collective-permute-start | bytes 2457608 | tf_op jit(solution)/shard_map/ppermute | solution.py:461
  68.7 5.5 %collective-permute-start.7 = (bf16[800,128]{1,0:T(8,128)(2,1)}, bf16[800,128]{1,0:T(8,128)(2,1)S(1)}, u32[]{:S(2)}, u32[]{:S(2)}) collective-permute-start(bf16[800,128]{1,0:T(8,128)(2,1)} %copy-done.18), channel_id=1, source_target_pairs={{0,16},{16,0},{1,17},{17,1},{2,18},{18,2},{3,19},{19,3},{4,20},{20... | collective-permute-start | bytes 614408 | tf_op jit(solution)/shard_map/ppermute | solution.py:465
  70.1 34.9 %copy-start.17 = (bf16[800,128]{1,0:T(8,128)(2,1)S(1)}, bf16[800,128]{1,0:T(8,128)(2,1)}, u32[]{:S(2)}) copy-start(bf16[800,128]{1,0:T(8,128)(2,1)} %shard_map.64.refs_6_) | copy-start | bytes 614404
  70.1 34.9 %copy-start.19 = (bf16[800,128]{1,0:T(8,128)(2,1)S(1)}, bf16[800,128]{1,0:T(8,128)(2,1)}, u32[]{:S(2)}) copy-start(bf16[800,128]{1,0:T(8,128)(2,1)} %copy-done.18) | copy-start | bytes 614404
  70.1 35.0 %copy-start.25 = (f32[256,1]{1,0:T(8,128)S(1)}, f32[256,1]{1,0:T(8,128)}, u32[]{:S(2)}) copy-start(f32[256,1]{1,0:T(8,128)} %get-tuple-element.231) | copy-start | bytes 3076
  70.1 35.0 %copy-start.26 = (s32[1,256]{1,0:T(1,128)S(1)}, s32[1,256]{1,0:T(1,128)}, u32[]{:S(2)}) copy-start(s32[1,256]{1,0:T(1,128)} %get-tuple-element.225) | copy-start | bytes 3076
  83.2 21.9 %copy-start.11 = (bf16[512,896]{1,0:T(8,128)(2,1)S(1)}, bf16[512,896]{1,0:T(8,128)(2,1)}, u32[]{:S(2)}) copy-start(bf16[512,896]{1,0:T(8,128)(2,1)} %get-tuple-element.222.refs_1_) | copy-start | bytes 2752516
  90.5 3.5 %collective-permute-start.11 = (f32[7,64,256]{2,1,0:T(8,128)S(1)}, f32[7,64,256]{2,1,0:T(8,128)S(1)}, u32[]{:S(2)}, u32[]{:S(2)}) collective-permute-start(f32[7,64,256]{2,1,0:T(8,128)S(1)} %get-tuple-element.228.own_ref), channel_id=1, source_target_pairs={{0,1},{1,0},{2,3},{3,2},{4,5},{5,4},{6,7},{7,6},{8,9},{9,8},{10,11... | collective-permute-start | bytes 1376264 | tf_op jit(solution)/shard_map/ppermute | solution.py:461
  90.6 14.4 %collective-permute-start.15 = (bf16[1600,128]{1,0:T(8,128)(2,1)}, bf16[1600,128]{1,0:T(8,128)(2,1)S(1)}, u32[]{:S(2)}, u32[]{:S(2)}) collective-permute-start(bf16[1600,128]{1,0:T(8,128)(2,1)} %collective-permute-done.2.refs_0_), channel_id=1, source_target_pairs={{0,16},{16,0},{1,17},{17,1},{2,18},{18,2},{3,19},{19,3},{4,20},{20... | collective-permute-start | bytes 1228808 | tf_op jit(solution)/shard_map/ppermute | solution.py:465
  94.1 10.9 %collective-permute-start.12 = (bf16[7,64,256]{2,1,0:T(8,128)(2,1)S(1)}, bf16[7,64,256]{2,1,0:T(8,128)(2,1)}, u32[]{:S(2)}, u32[]{:S(2)}) collective-permute-start(bf16[7,64,256]{2,1,0:T(8,128)(2,1)S(1)} %shard_map.66), channel_id=1, source_target_pairs={{0,2},{1,3},{2,0},{3,1},{4,6},{5,7},{6,4},{7,5},{8,10},{9,11},{10,... | collective-permute-start | bytes 688136 | tf_op jit(solution)/shard_map/ppermute | solution.py:461
  94.7 9.0 %collective-permute-start.10 = (bf16[1,1]{1,0:T(2,128)(2,1)}, bf16[1,1]{1,0:T(2,128)(2,1)}, u32[]{:S(2)}, u32[]{:S(2)}) collective-permute-start(bf16[1,1]{1,0:T(2,128)(2,1)} %slice.3), channel_id=1, source_target_pairs={{0,16},{16,0},{1,17},{17,1},{2,18},{18,2},{3,19},{19,3},{4,20},{20... | collective-permute-start | bytes 14 | tf_op jit(solution)/shard_map/ppermute | solution.py:465
  114.8 63.0 %all-to-all-start.1 = ((bf16[16,608,128]{2,1,0:T(8,128)(2,1)}), bf16[16,608,128]{2,1,0:T(8,128)(2,1)S(1)}, u32[]{:S(2)}, u32[]{:S(2)}) async-start(bf16[16,608,128]{2,1,0:T(8,128)(2,1)} %copy-done.3), calls=%async_computation.1 | async-start | bytes 4980736 | tf_op jit(solution)/shard_map/cond/branch_1_fun/all_to_all | solution.py:457
  (11 other events, 14.6 us)

commit v2 on v0

--- a/solution.py
+++ b/solution.py
@@ -270,7 +270,8 @@
 
         @pl.when(lax.rem(met_ref[a] // (1 << h), 2) > 0)
         def _(h=h, firsts=firsts):
-            step(near_refs[h] if h < 2 else opened_ref.at[h - 2], firsts)
+            is_first = lax.rem(met_ref[a], 1 << h) == 0
+            step(near_refs[h] if h < 2 else opened_ref.at[h - 2], firsts, is_first)
 
 
 def down_kernel(first_ref, rows_ref, *refs):
@@ -305,7 +306,7 @@
                 batch_ref[rows, tiles * LANES :] = pltpu.roll(end, shift, 1).astype(jnp.bfloat16)
             label = labels_ref[pl.ds(a, 1), :]
 
-            def step(weight_ref, firsts):
+            def step(weight_ref, firsts, is_first):
                 product = lax.dot_general(
                     weight_ref[...], batch_ref[...], dims, preferred_element_type=jnp.float32
                 )
@@ -357,16 +358,19 @@
         )
 
     def one(a, carry):
-        delta_ref[...] = jnp.zeros(delta_ref.shape, jnp.float32)
+        @pl.when(met_ref[a] == 0)
+        def _():
+            delta_ref[...] = jnp.zeros(delta_ref.shape, jnp.float32)
 
         @pl.when(met_ref[a] > 0)
         def _():
             label, twice = label_ref[a], twice_ref[a]
 
-            def step(weight_ref, firsts):
+            def step(weight_ref, firsts, is_first):
                 placed = [jnp.where(label == first, twice, 0.0) for first in firsts]
                 placed = jnp.concatenate(placed, axis=1).astype(jnp.bfloat16)
-                delta_ref[...] += jnp.dot(
+                before = jnp.where(is_first, 0.0, delta_ref[...])
+                delta_ref[...] = before + jnp.dot(
                     placed, weight_ref[...], preferred_element_type=jnp.float32
                 )
 
@@ -599,27 +603,32 @@
     first = jnp.concatenate([parts * resident, halves]).astype(i32)
     tiles = whole // LANES
 
-    def shares(weight, halved, after):
+    def shares(weight, which, halved, after):
         shapes = []
-        for k in range(QUAD):
+        for k in which:
             count = columns // 2 if k in halved else columns
             far = (count * tiles + count // QUAD, LANES)
             shapes.append(jax.ShapeDtypeStruct((columns, share) if k < 2 else far, bf16))
-        values = call(
-            functools.partial(weight_kernel, whole, range(QUAD), halved),
+        return call(
+            functools.partial(weight_kernel, whole, which, halved),
             shapes,
             [SMEM, SMEM, VMEM],
             0,
-            QUAD * columns * width,
+            len(which) * columns * width,
             after,
         )(parts, group.reshape(1), weight)
-        return [values[0]] + [towards(values[k], k, devices) for k in range(1, QUAD)]
-
-    weight = adapter_down_weight.transpose(0, 2, 1).reshape(columns, width)
-    down_weights = shares(weight, DOWN_HALVED, [])
-    weight = adapter_up_weight.reshape(columns, width)
-    up_weights = shares(weight, UP_HALVED, down_weights[:1])
-    down_weights[2] = stand_behind(down_weights[2], up_weights[0])
+
+    down_weight = adapter_down_weight.transpose(0, 2, 1).reshape(columns, width)
+    up_weight = adapter_up_weight.reshape(columns, width)
+    down_far = shares(down_weight, (2, 3), DOWN_HALVED, [])
+    up_far = shares(up_weight, (2, 3), UP_HALVED, down_far[:1])
+    down_near = shares(down_weight, (0, 1), (), up_far[:1])
+    up_near = shares(up_weight, (0, 1), (), down_near[:1])
+    down_weights = [down_near[0], towards(down_near[1], 1, devices)]
+    down_weights += [towards(value, k, devices) for k, value in zip((2, 3), down_far)]
+    up_weights = [up_near[0], towards(up_near[1], 1, devices)]
+    up_weights += [towards(value, k, devices) for k, value in zip((2, 3), up_far)]
+    down_weights[2] = stand_behind(down_weights[2], up_near[0])
     down_weights += [swapped(down_weights[k]) for k in DOWN_HALVED]
     up_weights += [swapped(up_weights[k]) for k in UP_HALVED]
 

time: 186 us -> 166 us (0.89)
  waiting for transfers between devices: 124 us -> 103 us
  starting transfers between devices: 19 us -> 27.1 us
  Pallas kernels: 32.2 us -> 27 us
    all_to_all x2, waiting for transfers between devices: 71.5 us -> 55.3 us  [exchange(): lax.all_to_all(value, 'adapter', split_axis=0, concat_axis=0, tiled=True)]
    ppermute x4, starting transfers between devices: 2.57 us -> 6.72 us  [swapped(): return lax.ppermute(value, 'groups', [(0, 1), (1, 0)])]
    all_to_all x2, starting transfers between devices: 11.9 us -> 15.9 us  [exchange(): lax.all_to_all(value, 'adapter', split_axis=0, concat_axis=0, tiled=True)]
    pallas_call x1, Pallas kernels: 10.3 us -> 6.57 us  [up_call(): call(up_kernel, jax.ShapeDtypeStruct(shape, jnp.bfloat16), [SMEM, SMEM] +...]
    ppermute x8, waiting for transfers between devices: 43.6 us -> 39.9 us  [towards(): return lax.ppermute(value, 'adapter', [(i, i ^ k) for i in range(devices)])]
    pallas_call x1, Pallas kernels: 10.7 us -> 7.33 us  [down_call(): call(down_kernel, [jax.ShapeDtypeStruct((cap // STEP, HALF, devices * STE...]
    pallas_call x2 -> x4, Pallas kernels: 5.22 us -> 7.17 us  [shares(): call(functools.partial(weight_kernel, whole, which, halved), shapes, [SME...]
    unnamed x20 -> x22, local copies, waits for them, and re-layouts: 5.36 us -> 5.34 us
  transfers between devices with their start and end apart: 14 -> 14, of which waited for: 7 -> 6; matrix products, arithmetic and copies ran while one was open for 1% -> 0% of each run, Pallas kernels for 9% -> 9%
where the time goes in v2:
time: 166 us
  waiting for transfers between devices  103 us (62%)
  starting transfers between devices  27.1 us (16%)
  Pallas kernels  27 us (16%)
  local copies, waits for them, and re-layouts  7.31 us (4%)
    all_to_all x2, waiting for transfers between devices, exchange(): lax.all_to_all(value, 'adapter', split_axis=0, concat_axis=0, tiled=True)  55.3 us
    ppermute x8, waiting for transfers between devices, towards(): return lax.ppermute(value, 'adapter', [(i, i ^ k) for i in range(devices)])  39.9 us
    all_to_all x2, starting transfers between devices, exchange(): lax.all_to_all(value, 'adapter', split_axis=0, concat_axis=0, tiled=True)  15.9 us
    pallas_call x1, Pallas kernels, down_call(): call(down_kernel, [jax.ShapeDtypeStruct((cap // STEP, HALF, devices * STE...  7.33 us
    ppermute x4, waiting for transfers between devices, swapped(): return lax.ppermute(value, 'groups', [(0, 1), (1, 0)])  7.31 us
    pallas_call x4, Pallas kernels, shares(): call(functools.partial(weight_kernel, whole, which, halved), shapes, [SME...  7.17 us
    ppermute x4, starting transfers between devices, swapped(): return lax.ppermute(value, 'groups', [(0, 1), (1, 0)])  6.72 us
    pallas_call x1, Pallas kernels, up_call(): call(up_kernel, jax.ShapeDtypeStruct(shape, jnp.bfloat16), [SMEM, SMEM] +...  6.57 us
  transfers between devices with their start and end apart: 14, of which 6 were waited for; matrix products, arithmetic and copies ran while one was open for 0% of the time, Pallas kernels for 9%

profile of v2, /device:TPU:11, one launch (start us, length us, event | category | flops | bytes accessed | tf_op | source)
XLA Modules:
  0.0 165.9 jit_solution(5217174957447773028)
XLA Ops:
  0.0 3.1 %shard_map.62 = (bf16[16,704,128]{2,1,0:T(8,128)(2,1)S(1)}, s32[1,256]{1,0:T(1,128)}, f32[256,1]{1,0:T(8,128)S(1)}) custom-call(s32[1,32]{1,0:T(1,128)} %bitcast.57, s32[1,32]{1,0:T(1,128)} %bitcast.56, bf16[256,3200]{1,0:T(8,128)(2,1)} %bitcast.35), custom_call_target="tpu_custom_call" | custom-call | flops 704643072 | bytes 4390912 | tf_op jit(solution)/shard_map/pallas_call | solution.py:479
  3.2 1.5 copy-done
  4.7 6.6 %all-to-all-start.9 = ((bf16[16,704,128]{2,1,0:T(8,128)(2,1)}), bf16[16,704,128]{2,1,0:T(8,128)(2,1)S(1)}, u32[]{:S(2)}, u32[]{:S(2)}) async-start(bf16[16,704,128]{2,1,0:T(8,128)(2,1)} %copy-done), calls=%async_computation.9 | async-start | bytes 5767168 | tf_op jit(solution)/shard_map/all_to_all | solution.py:455
  11.3 3.0 %shard_map.60 = (bf16[1600,128]{1,0:T(8,128)(2,1)S(1)}, bf16[1600,128]{1,0:T(8,128)(2,1)}) custom-call(s32[4]{0:T(128)S(1)} %iota_xor_fusion.part_ref.refs_1_, s32[1]{0:T(128)} %bitcast.20.group_ref.refs_2_, bf16[512,3200]{1,0:T(8,128)(2,1)} %bitcast.42), custom_call_target="tpu_custom_call" | custom-call | bytes 3276800 | tf_op jit(solution)/shard_map/pallas_call | solution.py:612
  16.1 1.6 shard_map.63
  18.4 1.5 collective-permute-start.5
  20.2 1.6 shard_map.64
  22.8 13.9 %collective-permute-done.4.refs_0_ = bf16[1600,128]{1,0:T(8,128)(2,1)S(1)} collective-permute-done((bf16[1600,128]{1,0:T(8,128)(2,1)S(1)}, bf16[1600,128]{1,0:T(8,128)(2,1)S(1)}, u32[]{:S(2)}, u32[]{:S(2)}) %collective-permute-start.4) | collective-permute-done | bytes 409632 | tf_op jit(solution)/shard_map/ppermute | solution.py:459
  37.5 1.2 collective-permute-start.6
  38.7 15.4 %collective-permute-done.5.refs_6_ = bf16[1600,128]{1,0:T(8,128)(2,1)} collective-permute-done((bf16[1600,128]{1,0:T(8,128)(2,1)}, bf16[1600,128]{1,0:T(8,128)(2,1)}, u32[]{:S(2)}, u32[]{:S(2)}) %collective-permute-start.5) | collective-permute-done | bytes 409632 | tf_op jit(solution)/shard_map/ppermute | solution.py:459
  54.1 1.2 collective-permute-start.7
  55.3 10.6 %collective-permute-done.2.refs_0_ = bf16[1600,128]{1,0:T(8,128)(2,1)} collective-permute-done((bf16[1600,128]{1,0:T(8,128)(2,1)S(1)}, bf16[1600,128]{1,0:T(8,128)(2,1)}, u32[]{:S(2)}, u32[]{:S(2)}) %collective-permute-start.2) | collective-permute-done | bytes 409632 | tf_op jit(solution)/shard_map/ppermute | solution.py:459
  66.0 1.9 %collective-permute-start.12 = (bf16[3200,128]{1,0:T(8,128)(2,1)}, bf16[3200,128]{1,0:T(8,128)(2,1)}, u32[]{:S(2)}, u32[]{:S(2)}) collective-permute-start(bf16[3200,128]{1,0:T(8,128)(2,1)} %copy-done.6), channel_id=1, source_target_pairs={{0,3},{1,2},{2,1},{3,0},{4,7},{5,6},{6,5},{7,4},{8,11},{9,10},{10,... | collective-permute-start | bytes 2457608 | tf_op jit(solution)/shard_map/ppermute | solution.py:459
  68.1 8.0 %all-to-all-done.9.refs_2_ = bf16[16,704,128]{2,1,0:T(8,128)(2,1)S(1)} async-done(((bf16[16,704,128]{2,1,0:T(8,128)(2,1)}), bf16[16,704,128]{2,1,0:T(8,128)(2,1)S(1)}, u32[]{:S(2)}, u32[]{:S(2)}) %all-to-all-start.9) | async-done | bytes 2883616 | tf_op jit(solution)/shard_map/all_to_all | solution.py:455
  76.1 7.3 %shard_map.66 = (f32[7,64,256]{2,1,0:T(8,128)S(1)}, bf16[16,128]{1,0:T(8,128)(2,1)S(1)}, bf16[256,128]{1,0:T(8,128)(2,1)S(1)}, s32[8]{0:T(128)S(1)}) custom-call(bf16[1600,128]{1,0:T(8,128)(2,1)} %collective-permute-done.2.refs_0_, s32[6]{0:T(128)S(1)} %pad_add_fusion.refs_1_, bf16[16,704,128]{2,1,0:T(8,128)(2,1)S(1)} %all-to-all-done.9.refs_2_, ...), custom_call_target="tpu_custom_call" | custom-call | tf_op jit(solution)/shard_map/pallas_call | solution.py:509
  83.5 2.5 %collective-permute-start.13 = (bf16[1600,128]{1,0:T(8,128)(2,1)}, bf16[1600,128]{1,0:T(8,128)(2,1)S(1)}, u32[]{:S(2)}, u32[]{:S(2)}) collective-permute-start(bf16[1600,128]{1,0:T(8,128)(2,1)} %collective-permute-done.2.refs_0_), channel_id=1, source_target_pairs={{0,16},{16,0},{1,17},{17,1},{2,18},{18,2},{3,19},{19,3},{4,20},{20... | collective-permute-start | bytes 1228808 | tf_op jit(solution)/shard_map/ppermute | solution.py:463
  86.7 1.7 %collective-permute-start.8 = (bf16[1,1]{1,0:T(2,128)(2,1)}, bf16[1,1]{1,0:T(2,128)(2,1)}, u32[]{:S(2)}, u32[]{:S(2)}) collective-permute-start(bf16[1,1]{1,0:T(2,128)(2,1)} %slice.3), channel_id=1, source_target_pairs={{0,16},{16,0},{1,17},{17,1},{2,18},{18,2},{3,19},{19,3},{4,20},{20... | collective-permute-start | bytes 14 | tf_op jit(solution)/shard_map/ppermute | solution.py:463
  88.4 7.3 %collective-permute-done.8 = bf16[1,1]{1,0:T(2,128)(2,1)} collective-permute-done((bf16[1,1]{1,0:T(2,128)(2,1)}, bf16[1,1]{1,0:T(2,128)(2,1)}, u32[]{:S(2)}, u32[]{:S(2)}) %collective-permute-start.8) | collective-permute-done | bytes 34 | tf_op jit(solution)/shard_map/ppermute | solution.py:463
  97.1 67.6 %conditional.1 = (bf16[32,8,3200]{2,1,0:T(8,128)(2,1)S(1)}) conditional(s32[]{:T(128)} %bitcast.29, (s32[1,256]{1,0:T(1,128)S(1)}, bf16[32,8,3200]{2,1,0:T(8,128)(2,1)}, s32[6]{0:T(128)S(1)}, s32[8]{0:T(128)S(1)}, bf16[256,128]{1,0:T(8,128)(2,1)S(1)}, /*index=5*/bf16[7,64,256]{2,1,0:T(8,128)(2,1)S(1)}, ...), branch_computations={%region_0.1_spmd, %region_1.2_spmd, %region_2.3_spmd, %region_3.4_... | conditional | flops 8422162432 | bytes 107582144 | solution.py:647
  97.2 6.6 %branch_0_fun.2 = bf16[16,512,128]{2,1,0:T(8,128)(2,1)S(1)} custom-call(s32[6]{0:T(128)S(1)} %get-tuple-element.132.first_ref, s32[8]{0:T(128)S(1)} %get-tuple-element.134.met_ref, bf16[256,128]{1,0:T(8,128)(2,1)S(1)} %get-tuple-element.135.notes_ref, bf16[7,64,256]{2,1,0:T(8,128)(2,1)S(1)} %get-tuple-element.136.refs_0_, ...), custom_call_target="tpu_custom_call" | custom-call | flops 4697620480 | bytes 8257536 | tf_op jit(solution)/shard_map/cond/branch_0_fun/pallas_call | solution.py:542
  103.7 1.3 copy-done.4
  105.1 9.3 %all-to-all-start = ((bf16[16,512,128]{2,1,0:T(8,128)(2,1)}), bf16[16,512,128]{2,1,0:T(8,128)(2,1)S(1)}, u32[]{:S(2)}, u32[]{:S(2)}) async-start(bf16[16,512,128]{2,1,0:T(8,128)(2,1)} %copy-done.4), calls=%async_computation | async-start | bytes 4194304 | tf_op jit(solution)/shard_map/cond/branch_0_fun/all_to_all | solution.py:455
  114.5 47.3 %all-to-all-done.refs_0_ = bf16[16,512,128]{2,1,0:T(8,128)(2,1)S(1)} async-done(((bf16[16,512,128]{2,1,0:T(8,128)(2,1)}), bf16[16,512,128]{2,1,0:T(8,128)(2,1)S(1)}, u32[]{:S(2)}, u32[]{:S(2)}) %all-to-all-start) | async-done | bytes 2097184 | tf_op jit(solution)/shard_map/cond/branch_0_fun/all_to_all | solution.py:455
  161.8 2.7 %branch_0_fun.3 = bf16[256,3200]{1,0:T(8,128)(2,1)S(1)} custom-call(s32[256,1]{1,0:T(8,128)S(1)} %copy.18.target_ref, bf16[256,3200]{1,0:T(8,128)(2,1)} %bitcast.36, bf16[16,512,128]{2,1,0:T(8,128)(2,1)S(1)} %all-to-all-done.refs_0_), custom_call_target="tpu_custom_call" | custom-call | flops 503316480 | bytes 5242880 | tf_op jit(solution)/shard_map/cond/branch_0_fun/pallas_call | solution.py:571
  (45 shorter events, 6.6 us)
Async XLA Ops:
  3.2 1.5 copy-start
  4.7 71.4 %all-to-all-start.9 = ((bf16[16,704,128]{2,1,0:T(8,128)(2,1)}), bf16[16,704,128]{2,1,0:T(8,128)(2,1)S(1)}, u32[]{:S(2)}, u32[]{:S(2)}) async-start(bf16[16,704,128]{2,1,0:T(8,128)(2,1)} %copy-done), calls=%async_computation.9 | async-start | bytes 5767168 | tf_op jit(solution)/shard_map/all_to_all | solution.py:455
  11.2 3.1 %copy-start.9 = (bf16[8,64,3200]{2,1,0:T(8,128)(2,1)S(1)}, bf16[8,64,3200]{2,1,0:T(8,128)(2,1)}, u32[]{:S(2)}) copy-start(bf16[8,64,3200]{2,1,0:T(8,128)(2,1)} %param.14) | copy-start | bytes 9830404
  11.3 4.8 %copy-start.8 = (bf16[8,3200,64]{1,2,0:T(8,128)(2,1)S(1)}, bf16[8,3200,64]{1,2,0:T(8,128)(2,1)}, u32[]{:S(2)}) copy-start(bf16[8,3200,64]{1,2,0:T(8,128)(2,1)} %param.13) | copy-start | bytes 9830404
  17.7 19.0 %copy-start.11 = (bf16[512,896]{1,0:T(8,128)(2,1)}, bf16[512,896]{1,0:T(8,128)(2,1)S(1)}, u32[]{:S(2)}) copy-start(bf16[512,896]{1,0:T(8,128)(2,1)S(1)} %get-tuple-element.212.refs_0_.refs_3_) | copy-start | bytes 2752516
  17.8 50.3 %collective-permute-start.3 = (bf16[512,896]{1,0:T(8,128)(2,1)}, bf16[512,896]{1,0:T(8,128)(2,1)}, u32[]{:S(2)}, u32[]{:S(2)}) collective-permute-start(bf16[512,896]{1,0:T(8,128)(2,1)} %get-tuple-element.213), channel_id=1, source_target_pairs={{0,1},{1,0},{2,3},{3,2},{4,5},{5,4},{6,7},{7,6},{8,9},{9,8},{10,11... | collective-permute-start | bytes 2752520 | tf_op jit(solution)/shard_map/ppermute | solution.py:459
  18.1 18.6 %collective-permute-start.4 = (bf16[1600,128]{1,0:T(8,128)(2,1)S(1)}, bf16[1600,128]{1,0:T(8,128)(2,1)S(1)}, u32[]{:S(2)}, u32[]{:S(2)}) collective-permute-start(bf16[1600,128]{1,0:T(8,128)(2,1)S(1)} %get-tuple-element.209.refs_0_), channel_id=1, source_target_pairs={{0,2},{1,3},{2,0},{3,1},{4,6},{5,7},{6,4},{7,5},{8,10},{9,11},{10,... | collective-permute-start | bytes 1228808 | tf_op jit(solution)/shard_map/ppermute | solution.py:459
  18.4 35.7 %collective-permute-start.5 = (bf16[1600,128]{1,0:T(8,128)(2,1)}, bf16[1600,128]{1,0:T(8,128)(2,1)}, u32[]{:S(2)}, u32[]{:S(2)}) collective-permute-start(bf16[1600,128]{1,0:T(8,128)(2,1)} %get-tuple-element.215), channel_id=1, source_target_pairs={{0,3},{1,2},{2,1},{3,0},{4,7},{5,6},{6,5},{7,4},{8,11},{9,10},{10,... | collective-permute-start | bytes 1228808 | tf_op jit(solution)/shard_map/ppermute | solution.py:459
  19.9 46.1 %collective-permute-start.2 = (bf16[1600,128]{1,0:T(8,128)(2,1)S(1)}, bf16[1600,128]{1,0:T(8,128)(2,1)}, u32[]{:S(2)}, u32[]{:S(2)}) collective-permute-start(bf16[1600,128]{1,0:T(8,128)(2,1)S(1)} %get-tuple-element.210.refs_0_), channel_id=1, source_target_pairs={{0,2},{1,3},{2,0},{3,1},{4,6},{5,7},{6,4},{7,5},{8,10},{9,11},{10,... | collective-permute-start | bytes 1228808 | tf_op jit(solution)/shard_map/ppermute | solution.py:459
  21.8 1.0 copy-start.5
  37.5 30.6 %collective-permute-start.6 = (bf16[1600,128]{1,0:T(8,128)(2,1)}, bf16[1600,128]{1,0:T(8,128)(2,1)}, u32[]{:S(2)}, u32[]{:S(2)}) collective-permute-start(bf16[1600,128]{1,0:T(8,128)(2,1)} %shard_map.65.refs_5_), channel_id=1, source_target_pairs={{0,16},{16,0},{1,17},{17,1},{2,18},{18,2},{3,19},{19,3},{4,20},{20... | collective-permute-start | bytes 1228808 | tf_op jit(solution)/shard_map/ppermute | solution.py:463
  54.1 14.0 %collective-permute-start.7 = (bf16[1600,128]{1,0:T(8,128)(2,1)}, bf16[1600,128]{1,0:T(8,128)(2,1)}, u32[]{:S(2)}, u32[]{:S(2)}) collective-permute-start(bf16[1600,128]{1,0:T(8,128)(2,1)} %collective-permute-done.5.refs_6_), channel_id=1, source_target_pairs={{0,16},{16,0},{1,17},{17,1},{2,18},{18,2},{3,19},{19,3},{4,20},{20... | collective-permute-start | bytes 1228808 | tf_op jit(solution)/shard_map/ppermute | solution.py:463
  55.3 41.8 %collective-permute-start.11 = (bf16[512,896]{1,0:T(8,128)(2,1)}, bf16[512,896]{1,0:T(8,128)(2,1)}, u32[]{:S(2)}, u32[]{:S(2)}) collective-permute-start(bf16[512,896]{1,0:T(8,128)(2,1)} %copy-done.5), channel_id=1, source_target_pairs={{0,1},{1,0},{2,3},{3,2},{4,5},{5,4},{6,7},{7,6},{8,9},{9,8},{10,11... | collective-permute-start | bytes 2752520 | tf_op jit(solution)/shard_map/ppermute | solution.py:459
  66.0 31.1 %collective-permute-start.12 = (bf16[3200,128]{1,0:T(8,128)(2,1)}, bf16[3200,128]{1,0:T(8,128)(2,1)}, u32[]{:S(2)}, u32[]{:S(2)}) collective-permute-start(bf16[3200,128]{1,0:T(8,128)(2,1)} %copy-done.6), channel_id=1, source_target_pairs={{0,3},{1,2},{2,1},{3,0},{4,7},{5,6},{6,5},{7,4},{8,11},{9,10},{10,... | collective-permute-start | bytes 2457608 | tf_op jit(solution)/shard_map/ppermute | solution.py:459
  68.1 29.0 %copy-start.14 = (bf16[1600,128]{1,0:T(8,128)(2,1)S(1)}, bf16[1600,128]{1,0:T(8,128)(2,1)}, u32[]{:S(2)}) copy-start(bf16[1600,128]{1,0:T(8,128)(2,1)} %shard_map.65.refs_5_) | copy-start | bytes 1228804
  68.1 29.1 %copy-start.20 = (s32[1,256]{1,0:T(1,128)S(1)}, s32[1,256]{1,0:T(1,128)}, u32[]{:S(2)}) copy-start(s32[1,256]{1,0:T(1,128)} %get-tuple-element.217) | copy-start | bytes 3076
  76.1 21.0 %copy-start.15 = (bf16[512,896]{1,0:T(8,128)(2,1)S(1)}, bf16[512,896]{1,0:T(8,128)(2,1)}, u32[]{:S(2)}) copy-start(bf16[512,896]{1,0:T(8,128)(2,1)} %get-tuple-element.214.refs_1_) | copy-start | bytes 2752516
  83.4 2.6 %collective-permute-start.9 = (f32[7,64,256]{2,1,0:T(8,128)S(1)}, f32[7,64,256]{2,1,0:T(8,128)S(1)}, u32[]{:S(2)}, u32[]{:S(2)}) collective-permute-start(f32[7,64,256]{2,1,0:T(8,128)S(1)} %get-tuple-element.220.own_ref), channel_id=1, source_target_pairs={{0,1},{1,0},{2,3},{3,2},{4,5},{5,4},{6,7},{7,6},{8,9},{9,8},{10,11... | collective-permute-start | bytes 1376264 | tf_op jit(solution)/shard_map/ppermute | solution.py:459
  83.5 13.6 %collective-permute-start.13 = (bf16[1600,128]{1,0:T(8,128)(2,1)}, bf16[1600,128]{1,0:T(8,128)(2,1)S(1)}, u32[]{:S(2)}, u32[]{:S(2)}) collective-permute-start(bf16[1600,128]{1,0:T(8,128)(2,1)} %collective-permute-done.2.refs_0_), channel_id=1, source_target_pairs={{0,16},{16,0},{1,17},{17,1},{2,18},{18,2},{3,19},{19,3},{4,20},{20... | collective-permute-start | bytes 1228808 | tf_op jit(solution)/shard_map/ppermute | solution.py:463
  86.1 11.0 %collective-permute-start.10 = (bf16[7,64,256]{2,1,0:T(8,128)(2,1)S(1)}, bf16[7,64,256]{2,1,0:T(8,128)(2,1)S(1)}, u32[]{:S(2)}, u32[]{:S(2)}) collective-permute-start(bf16[7,64,256]{2,1,0:T(8,128)(2,1)S(1)} %shard_map.67), channel_id=1, source_target_pairs={{0,2},{1,3},{2,0},{3,1},{4,6},{5,7},{6,4},{7,5},{8,10},{9,11},{10,... | collective-permute-start | bytes 688136 | tf_op jit(solution)/shard_map/ppermute | solution.py:459
  86.7 9.0 %collective-permute-start.8 = (bf16[1,1]{1,0:T(2,128)(2,1)}, bf16[1,1]{1,0:T(2,128)(2,1)}, u32[]{:S(2)}, u32[]{:S(2)}) collective-permute-start(bf16[1,1]{1,0:T(2,128)(2,1)} %slice.3), channel_id=1, source_target_pairs={{0,16},{16,0},{1,17},{17,1},{2,18},{18,2},{3,19},{19,3},{4,20},{20... | collective-permute-start | bytes 14 | tf_op jit(solution)/shard_map/ppermute | solution.py:463
  103.7 1.3 copy-start.4
  105.1 56.7 %all-to-all-start = ((bf16[16,512,128]{2,1,0:T(8,128)(2,1)}), bf16[16,512,128]{2,1,0:T(8,128)(2,1)S(1)}, u32[]{:S(2)}, u32[]{:S(2)}) async-start(bf16[16,512,128]{2,1,0:T(8,128)(2,1)} %copy-done.4), calls=%async_computation | async-start | bytes 4194304 | tf_op jit(solution)/shard_map/cond/branch_0_fun/all_to_all | solution.py:455
  164.7 1.2 copy-start.19
  (2 other events, 1.7 us)

commit v3 on v2

--- a/solution.py
+++ b/solution.py
@@ -445,7 +445,7 @@
         in_specs=[pl.BlockSpec(memory_space=pl.ANY)] * skipped + in_specs,
         out_specs=out_specs or ([VMEM] * len(out_shape) if many else VMEM),
         scratch_shapes=scratch,
-        compiler_params=pltpu.CompilerParams(vmem_limit_bytes=48 * 2**20),
+        compiler_params=pltpu.CompilerParams(vmem_limit_bytes=28 * 2**20),
         cost_estimate=pl.CostEstimate(flops=flops, bytes_accessed=moved, transcendentals=0),
     )
     return functools.partial(run, *after)

time: 166 us -> 165 us (level)
  transfers between devices with their start and end apart: 14 -> 14, of which waited for: 6 -> 6; matrix products, arithmetic and copies ran while one was open for 0% -> 0% of each run, Pallas kernels for 9% -> 8%
where the time goes in v3:
time: 165 us; the launch traced here: 164 us
  waiting for transfers between devices  103 us (62%)
  starting transfers between devices  26.6 us (16%)
  Pallas kernels  26 us (16%)
  local copies, waits for them, and re-layouts  7.31 us (4%)
    all_to_all x2, waiting for transfers between devices, exchange(): lax.all_to_all(value, 'adapter', split_axis=0, concat_axis=0, tiled=True)  55.3 us
    ppermute x8, waiting for transfers between devices, towards(): return lax.ppermute(value, 'adapter', [(i, i ^ k) for i in range(devices)])  39.9 us
    all_to_all x2, starting transfers between devices, exchange(): lax.all_to_all(value, 'adapter', split_axis=0, concat_axis=0, tiled=True)  14.7 us
    ppermute x4, starting transfers between devices, swapped(): return lax.ppermute(value, 'groups', [(0, 1), (1, 0)])  7.33 us
    ppermute x4, waiting for transfers between devices, swapped(): return lax.ppermute(value, 'groups', [(0, 1), (1, 0)])  7.31 us
    pallas_call x4, Pallas kernels, shares(): call(functools.partial(weight_kernel, whole, which, halved), shapes, [SME...  7.17 us
    pallas_call x1, Pallas kernels, down_call(): call(down_kernel, [jax.ShapeDtypeStruct((cap // STEP, HALF, devices * STE...  6.73 us
    pallas_call x1, Pallas kernels, up_call(): call(up_kernel, jax.ShapeDtypeStruct(shape, jnp.bfloat16), [SMEM, SMEM] +...  6.12 us
  transfers between devices with their start and end apart: 14, of which 6 were waited for; matrix products, arithmetic and copies ran while one was open for 0% of the time, Pallas kernels for 8%

profile of v3, /device:TPU:11, one launch (start us, length us, event | category | flops | bytes accessed | tf_op | source)
XLA Modules:
  0.0 164.3 jit_solution(15755639134722364630)
XLA Ops:
  0.0 3.1 %shard_map.62 = (bf16[16,704,128]{2,1,0:T(8,128)(2,1)S(1)}, s32[1,256]{1,0:T(1,128)}, f32[256,1]{1,0:T(8,128)S(1)}) custom-call(s32[1,32]{1,0:T(1,128)} %bitcast.57, s32[1,32]{1,0:T(1,128)} %bitcast.56, bf16[256,3200]{1,0:T(8,128)(2,1)} %bitcast.35), custom_call_target="tpu_custom_call" | custom-call | flops 704643072 | bytes 4390912 | tf_op jit(solution)/shard_map/pallas_call | solution.py:479
  3.2 1.5 copy-done
  4.7 6.6 %all-to-all-start.9 = ((bf16[16,704,128]{2,1,0:T(8,128)(2,1)}), bf16[16,704,128]{2,1,0:T(8,128)(2,1)S(1)}, u32[]{:S(2)}, u32[]{:S(2)}) async-start(bf16[16,704,128]{2,1,0:T(8,128)(2,1)} %copy-done), calls=%async_computation.9 | async-start | bytes 5767168 | tf_op jit(solution)/shard_map/all_to_all | solution.py:455
  11.3 3.0 %shard_map.60 = (bf16[1600,128]{1,0:T(8,128)(2,1)S(1)}, bf16[1600,128]{1,0:T(8,128)(2,1)}) custom-call(s32[4]{0:T(128)S(1)} %iota_xor_fusion.part_ref.refs_1_, s32[1]{0:T(128)} %bitcast.20.group_ref.refs_2_, bf16[512,3200]{1,0:T(8,128)(2,1)} %bitcast.42), custom_call_target="tpu_custom_call" | custom-call | bytes 3276800 | tf_op jit(solution)/shard_map/pallas_call | solution.py:612
  16.1 1.6 shard_map.63
  18.4 1.5 collective-permute-start.5
  20.2 1.6 shard_map.64
  22.8 13.9 %collective-permute-done.4.refs_0_ = bf16[1600,128]{1,0:T(8,128)(2,1)S(1)} collective-permute-done((bf16[1600,128]{1,0:T(8,128)(2,1)S(1)}, bf16[1600,128]{1,0:T(8,128)(2,1)S(1)}, u32[]{:S(2)}, u32[]{:S(2)}) %collective-permute-start.4) | collective-permute-done | bytes 409632 | tf_op jit(solution)/shard_map/ppermute | solution.py:459
  37.5 1.2 collective-permute-start.6
  38.7 15.4 %collective-permute-done.5.refs_6_ = bf16[1600,128]{1,0:T(8,128)(2,1)} collective-permute-done((bf16[1600,128]{1,0:T(8,128)(2,1)}, bf16[1600,128]{1,0:T(8,128)(2,1)}, u32[]{:S(2)}, u32[]{:S(2)}) %collective-permute-start.5) | collective-permute-done | bytes 409632 | tf_op jit(solution)/shard_map/ppermute | solution.py:459
  54.1 1.2 collective-permute-start.7
  55.3 10.6 %collective-permute-done.2.refs_0_ = bf16[1600,128]{1,0:T(8,128)(2,1)} collective-permute-done((bf16[1600,128]{1,0:T(8,128)(2,1)S(1)}, bf16[1600,128]{1,0:T(8,128)(2,1)}, u32[]{:S(2)}, u32[]{:S(2)}) %collective-permute-start.2) | collective-permute-done | bytes 409632 | tf_op jit(solution)/shard_map/ppermute | solution.py:459
  66.0 1.9 %collective-permute-start.12 = (bf16[3200,128]{1,0:T(8,128)(2,1)}, bf16[3200,128]{1,0:T(8,128)(2,1)}, u32[]{:S(2)}, u32[]{:S(2)}) collective-permute-start(bf16[3200,128]{1,0:T(8,128)(2,1)} %copy-done.6), channel_id=1, source_target_pairs={{0,3},{1,2},{2,1},{3,0},{4,7},{5,6},{6,5},{7,4},{8,11},{9,10},{10,... | collective-permute-start | bytes 2457608 | tf_op jit(solution)/shard_map/ppermute | solution.py:459
  68.1 8.0 %all-to-all-done.9.refs_2_ = bf16[16,704,128]{2,1,0:T(8,128)(2,1)S(1)} async-done(((bf16[16,704,128]{2,1,0:T(8,128)(2,1)}), bf16[16,704,128]{2,1,0:T(8,128)(2,1)S(1)}, u32[]{:S(2)}, u32[]{:S(2)}) %all-to-all-start.9) | async-done | bytes 2883616 | tf_op jit(solution)/shard_map/all_to_all | solution.py:455
  76.1 6.7 %shard_map.66 = (f32[7,64,256]{2,1,0:T(8,128)S(1)}, bf16[16,128]{1,0:T(8,128)(2,1)S(1)}, bf16[256,128]{1,0:T(8,128)(2,1)S(1)}, s32[8]{0:T(128)S(1)}) custom-call(bf16[1600,128]{1,0:T(8,128)(2,1)} %collective-permute-done.2.refs_0_, s32[6]{0:T(128)S(1)} %pad_add_fusion.refs_1_, bf16[16,704,128]{2,1,0:T(8,128)(2,1)S(1)} %all-to-all-done.9.refs_2_, ...), custom_call_target="tpu_custom_call" | custom-call | tf_op jit(solution)/shard_map/pallas_call | solution.py:509
  82.9 3.1 %collective-permute-start.13 = (bf16[1600,128]{1,0:T(8,128)(2,1)}, bf16[1600,128]{1,0:T(8,128)(2,1)S(1)}, u32[]{:S(2)}, u32[]{:S(2)}) collective-permute-start(bf16[1600,128]{1,0:T(8,128)(2,1)} %collective-permute-done.2.refs_0_), channel_id=1, source_target_pairs={{0,16},{16,0},{1,17},{17,1},{2,18},{18,2},{3,19},{19,3},{4,20},{20... | collective-permute-start | bytes 1228808 | tf_op jit(solution)/shard_map/ppermute | solution.py:463
  86.7 1.7 %collective-permute-start.8 = (bf16[1,1]{1,0:T(2,128)(2,1)}, bf16[1,1]{1,0:T(2,128)(2,1)}, u32[]{:S(2)}, u32[]{:S(2)}) collective-permute-start(bf16[1,1]{1,0:T(2,128)(2,1)} %slice.3), channel_id=1, source_target_pairs={{0,16},{16,0},{1,17},{17,1},{2,18},{18,2},{3,19},{19,3},{4,20},{20... | collective-permute-start | bytes 14 | tf_op jit(solution)/shard_map/ppermute | solution.py:463
  88.4 7.3 %collective-permute-done.8 = bf16[1,1]{1,0:T(2,128)(2,1)} collective-permute-done((bf16[1,1]{1,0:T(2,128)(2,1)}, bf16[1,1]{1,0:T(2,128)(2,1)}, u32[]{:S(2)}, u32[]{:S(2)}) %collective-permute-start.8) | collective-permute-done | bytes 34 | tf_op jit(solution)/shard_map/ppermute | solution.py:463
  97.2 66.0 %conditional.1 = (bf16[32,8,3200]{2,1,0:T(8,128)(2,1)S(1)}) conditional(s32[]{:T(128)} %bitcast.29, (s32[1,256]{1,0:T(1,128)S(1)}, bf16[32,8,3200]{2,1,0:T(8,128)(2,1)}, s32[6]{0:T(128)S(1)}, s32[8]{0:T(128)S(1)}, bf16[256,128]{1,0:T(8,128)(2,1)S(1)}, /*index=5*/bf16[7,64,256]{2,1,0:T(8,128)(2,1)S(1)}, ...), branch_computations={%region_0.1_spmd, %region_1.2_spmd, %region_2.3_spmd, %region_3.4_... | conditional | flops 8422162432 | bytes 107582144 | solution.py:647
  97.2 6.1 %branch_0_fun.2 = bf16[16,512,128]{2,1,0:T(8,128)(2,1)S(1)} custom-call(s32[6]{0:T(128)S(1)} %get-tuple-element.132.first_ref, s32[8]{0:T(128)S(1)} %get-tuple-element.134.met_ref, bf16[256,128]{1,0:T(8,128)(2,1)S(1)} %get-tuple-element.135.notes_ref, bf16[7,64,256]{2,1,0:T(8,128)(2,1)S(1)} %get-tuple-element.136.refs_0_, ...), custom_call_target="tpu_custom_call" | custom-call | flops 4697620480 | bytes 8257536 | tf_op jit(solution)/shard_map/cond/branch_0_fun/pallas_call | solution.py:542
  103.3 1.3 copy-done.4
  104.6 8.2 %all-to-all-start = ((bf16[16,512,128]{2,1,0:T(8,128)(2,1)}), bf16[16,512,128]{2,1,0:T(8,128)(2,1)S(1)}, u32[]{:S(2)}, u32[]{:S(2)}) async-start(bf16[16,512,128]{2,1,0:T(8,128)(2,1)} %copy-done.4), calls=%async_computation | async-start | bytes 4194304 | tf_op jit(solution)/shard_map/cond/branch_0_fun/all_to_all | solution.py:455
  112.9 47.3 %all-to-all-done.refs_0_ = bf16[16,512,128]{2,1,0:T(8,128)(2,1)S(1)} async-done(((bf16[16,512,128]{2,1,0:T(8,128)(2,1)}), bf16[16,512,128]{2,1,0:T(8,128)(2,1)S(1)}, u32[]{:S(2)}, u32[]{:S(2)}) %all-to-all-start) | async-done | bytes 2097184 | tf_op jit(solution)/shard_map/cond/branch_0_fun/all_to_all | solution.py:455
  160.2 2.7 %branch_0_fun.3 = bf16[256,3200]{1,0:T(8,128)(2,1)S(1)} custom-call(s32[256,1]{1,0:T(8,128)S(1)} %copy.18.target_ref, bf16[256,3200]{1,0:T(8,128)(2,1)} %bitcast.36, bf16[16,512,128]{2,1,0:T(8,128)(2,1)S(1)} %all-to-all-done.refs_0_), custom_call_target="tpu_custom_call" | custom-call | flops 503316480 | bytes 5242880 | tf_op jit(solution)/shard_map/cond/branch_0_fun/pallas_call | solution.py:571
  (45 shorter events, 6.6 us)
Async XLA Ops:
  3.2 1.5 copy-start
  4.7 71.4 %all-to-all-start.9 = ((bf16[16,704,128]{2,1,0:T(8,128)(2,1)}), bf16[16,704,128]{2,1,0:T(8,128)(2,1)S(1)}, u32[]{:S(2)}, u32[]{:S(2)}) async-start(bf16[16,704,128]{2,1,0:T(8,128)(2,1)} %copy-done), calls=%async_computation.9 | async-start | bytes 5767168 | tf_op jit(solution)/shard_map/all_to_all | solution.py:455
  11.2 3.1 %copy-start.9 = (bf16[8,64,3200]{2,1,0:T(8,128)(2,1)S(1)}, bf16[8,64,3200]{2,1,0:T(8,128)(2,1)}, u32[]{:S(2)}) copy-start(bf16[8,64,3200]{2,1,0:T(8,128)(2,1)} %param.14) | copy-start | bytes 9830404
  11.3 4.8 %copy-start.8 = (bf16[8,3200,64]{1,2,0:T(8,128)(2,1)S(1)}, bf16[8,3200,64]{1,2,0:T(8,128)(2,1)}, u32[]{:S(2)}) copy-start(bf16[8,3200,64]{1,2,0:T(8,128)(2,1)} %param.13) | copy-start | bytes 9830404
  17.7 19.0 %copy-start.11 = (bf16[512,896]{1,0:T(8,128)(2,1)}, bf16[512,896]{1,0:T(8,128)(2,1)S(1)}, u32[]{:S(2)}) copy-start(bf16[512,896]{1,0:T(8,128)(2,1)S(1)} %get-tuple-element.212.refs_0_.refs_3_) | copy-start | bytes 2752516
  17.8 50.3 %collective-permute-start.3 = (bf16[512,896]{1,0:T(8,128)(2,1)}, bf16[512,896]{1,0:T(8,128)(2,1)}, u32[]{:S(2)}, u32[]{:S(2)}) collective-permute-start(bf16[512,896]{1,0:T(8,128)(2,1)} %get-tuple-element.213), channel_id=1, source_target_pairs={{0,1},{1,0},{2,3},{3,2},{4,5},{5,4},{6,7},{7,6},{8,9},{9,8},{10,11... | collective-permute-start | bytes 2752520 | tf_op jit(solution)/shard_map/ppermute | solution.py:459
  18.1 18.6 %collective-permute-start.4 = (bf16[1600,128]{1,0:T(8,128)(2,1)S(1)}, bf16[1600,128]{1,0:T(8,128)(2,1)S(1)}, u32[]{:S(2)}, u32[]{:S(2)}) collective-permute-start(bf16[1600,128]{1,0:T(8,128)(2,1)S(1)} %get-tuple-element.209.refs_0_), channel_id=1, source_target_pairs={{0,2},{1,3},{2,0},{3,1},{4,6},{5,7},{6,4},{7,5},{8,10},{9,11},{10,... | collective-permute-start | bytes 1228808 | tf_op jit(solution)/shard_map/ppermute | solution.py:459
  18.4 35.7 %collective-permute-start.5 = (bf16[1600,128]{1,0:T(8,128)(2,1)}, bf16[1600,128]{1,0:T(8,128)(2,1)}, u32[]{:S(2)}, u32[]{:S(2)}) collective-permute-start(bf16[1600,128]{1,0:T(8,128)(2,1)} %get-tuple-element.215), channel_id=1, source_target_pairs={{0,3},{1,2},{2,1},{3,0},{4,7},{5,6},{6,5},{7,4},{8,11},{9,10},{10,... | collective-permute-start | bytes 1228808 | tf_op jit(solution)/shard_map/ppermute | solution.py:459
  19.9 46.1 %collective-permute-start.2 = (bf16[1600,128]{1,0:T(8,128)(2,1)S(1)}, bf16[1600,128]{1,0:T(8,128)(2,1)}, u32[]{:S(2)}, u32[]{:S(2)}) collective-permute-start(bf16[1600,128]{1,0:T(8,128)(2,1)S(1)} %get-tuple-element.210.refs_0_), channel_id=1, source_target_pairs={{0,2},{1,3},{2,0},{3,1},{4,6},{5,7},{6,4},{7,5},{8,10},{9,11},{10,... | collective-permute-start | bytes 1228808 | tf_op jit(solution)/shard_map/ppermute | solution.py:459
  21.8 1.0 copy-start.5
  37.5 30.6 %collective-permute-start.6 = (bf16[1600,128]{1,0:T(8,128)(2,1)}, bf16[1600,128]{1,0:T(8,128)(2,1)}, u32[]{:S(2)}, u32[]{:S(2)}) collective-permute-start(bf16[1600,128]{1,0:T(8,128)(2,1)} %shard_map.65.refs_5_), channel_id=1, source_target_pairs={{0,16},{16,0},{1,17},{17,1},{2,18},{18,2},{3,19},{19,3},{4,20},{20... | collective-permute-start | bytes 1228808 | tf_op jit(solution)/shard_map/ppermute | solution.py:463
  54.1 14.0 %collective-permute-start.7 = (bf16[1600,128]{1,0:T(8,128)(2,1)}, bf16[1600,128]{1,0:T(8,128)(2,1)}, u32[]{:S(2)}, u32[]{:S(2)}) collective-permute-start(bf16[1600,128]{1,0:T(8,128)(2,1)} %collective-permute-done.5.refs_6_), channel_id=1, source_target_pairs={{0,16},{16,0},{1,17},{17,1},{2,18},{18,2},{3,19},{19,3},{4,20},{20... | collective-permute-start | bytes 1228808 | tf_op jit(solution)/shard_map/ppermute | solution.py:463
  55.3 41.8 %collective-permute-start.11 = (bf16[512,896]{1,0:T(8,128)(2,1)}, bf16[512,896]{1,0:T(8,128)(2,1)}, u32[]{:S(2)}, u32[]{:S(2)}) collective-permute-start(bf16[512,896]{1,0:T(8,128)(2,1)} %copy-done.5), channel_id=1, source_target_pairs={{0,1},{1,0},{2,3},{3,2},{4,5},{5,4},{6,7},{7,6},{8,9},{9,8},{10,11... | collective-permute-start | bytes 2752520 | tf_op jit(solution)/shard_map/ppermute | solution.py:459
  66.0 31.1 %collective-permute-start.12 = (bf16[3200,128]{1,0:T(8,128)(2,1)}, bf16[3200,128]{1,0:T(8,128)(2,1)}, u32[]{:S(2)}, u32[]{:S(2)}) collective-permute-start(bf16[3200,128]{1,0:T(8,128)(2,1)} %copy-done.6), channel_id=1, source_target_pairs={{0,3},{1,2},{2,1},{3,0},{4,7},{5,6},{6,5},{7,4},{8,11},{9,10},{10,... | collective-permute-start | bytes 2457608 | tf_op jit(solution)/shard_map/ppermute | solution.py:459
  68.1 29.1 %copy-start.14 = (bf16[1600,128]{1,0:T(8,128)(2,1)S(1)}, bf16[1600,128]{1,0:T(8,128)(2,1)}, u32[]{:S(2)}) copy-start(bf16[1600,128]{1,0:T(8,128)(2,1)} %shard_map.65.refs_5_) | copy-start | bytes 1228804
  68.1 29.1 %copy-start.20 = (s32[1,256]{1,0:T(1,128)S(1)}, s32[1,256]{1,0:T(1,128)}, u32[]{:S(2)}) copy-start(s32[1,256]{1,0:T(1,128)} %get-tuple-element.217) | copy-start | bytes 3076
  76.1 21.1 %copy-start.15 = (bf16[512,896]{1,0:T(8,128)(2,1)S(1)}, bf16[512,896]{1,0:T(8,128)(2,1)}, u32[]{:S(2)}) copy-start(bf16[512,896]{1,0:T(8,128)(2,1)} %get-tuple-element.214.refs_1_) | copy-start | bytes 2752516
  82.8 3.2 %collective-permute-start.9 = (f32[7,64,256]{2,1,0:T(8,128)S(1)}, f32[7,64,256]{2,1,0:T(8,128)S(1)}, u32[]{:S(2)}, u32[]{:S(2)}) collective-permute-start(f32[7,64,256]{2,1,0:T(8,128)S(1)} %get-tuple-element.220.own_ref), channel_id=1, source_target_pairs={{0,1},{1,0},{2,3},{3,2},{4,5},{5,4},{6,7},{7,6},{8,9},{9,8},{10,11... | collective-permute-start | bytes 1376264 | tf_op jit(solution)/shard_map/ppermute | solution.py:459
  82.9 14.2 %collective-permute-start.13 = (bf16[1600,128]{1,0:T(8,128)(2,1)}, bf16[1600,128]{1,0:T(8,128)(2,1)S(1)}, u32[]{:S(2)}, u32[]{:S(2)}) collective-permute-start(bf16[1600,128]{1,0:T(8,128)(2,1)} %collective-permute-done.2.refs_0_), channel_id=1, source_target_pairs={{0,16},{16,0},{1,17},{17,1},{2,18},{18,2},{3,19},{19,3},{4,20},{20... | collective-permute-start | bytes 1228808 | tf_op jit(solution)/shard_map/ppermute | solution.py:463
  86.1 11.0 %collective-permute-start.10 = (bf16[7,64,256]{2,1,0:T(8,128)(2,1)S(1)}, bf16[7,64,256]{2,1,0:T(8,128)(2,1)S(1)}, u32[]{:S(2)}, u32[]{:S(2)}) collective-permute-start(bf16[7,64,256]{2,1,0:T(8,128)(2,1)S(1)} %shard_map.67), channel_id=1, source_target_pairs={{0,2},{1,3},{2,0},{3,1},{4,6},{5,7},{6,4},{7,5},{8,10},{9,11},{10,... | collective-permute-start | bytes 688136 | tf_op jit(solution)/shard_map/ppermute | solution.py:459
  86.7 9.0 %collective-permute-start.8 = (bf16[1,1]{1,0:T(2,128)(2,1)}, bf16[1,1]{1,0:T(2,128)(2,1)}, u32[]{:S(2)}, u32[]{:S(2)}) collective-permute-start(bf16[1,1]{1,0:T(2,128)(2,1)} %slice.3), channel_id=1, source_target_pairs={{0,16},{16,0},{1,17},{17,1},{2,18},{18,2},{3,19},{19,3},{4,20},{20... | collective-permute-start | bytes 14 | tf_op jit(solution)/shard_map/ppermute | solution.py:463
  103.3 1.3 copy-start.4
  104.6 55.6 %all-to-all-start = ((bf16[16,512,128]{2,1,0:T(8,128)(2,1)}), bf16[16,512,128]{2,1,0:T(8,128)(2,1)S(1)}, u32[]{:S(2)}, u32[]{:S(2)}) async-start(bf16[16,512,128]{2,1,0:T(8,128)(2,1)} %copy-done.4), calls=%async_computation | async-start | bytes 4194304 | tf_op jit(solution)/shard_map/cond/branch_0_fun/all_to_all | solution.py:455
  163.1 1.2 copy-start.19
  (2 other events, 1.7 us)
